TPU v7x, 32 devices: a whole 2x2x4 slice. The times are simulated.
32 devices in a mesh: mod: 2 (over y), dp: 16 (over z, x, core).
Axes of the slice: x: 2, y: 2, z: 4, core: 2. Of those that a mesh axis runs over, the one named last changes fastest.
Arguments:
- text_tokens: bfloat16 [24576, 768], P(('mod', 'dp')), may hold values from -6 to 6
- patches: bfloat16 [192, 145, 1024], P(('mod', 'dp')), may hold values from -6 to 6
- lengths: int32 [32, 24], P(('mod', 'dp')), may hold values from 1 to 40, 768 in all within a row
- row_image: int32 [32, 24], P(('mod', 'dp')), may hold values from 0 to 5
- box_mask: int32 [32, 24, 145], P(('mod', 'dp')), may hold values from 0 to 1, as said below
- cotangent: bfloat16 [24576, 768], P(('mod', 'dp')), may hold values from -6 to 6
- self_query: bfloat16 [768, 768], replicated, may hold values from -0.21875 to 0.21875
- self_key: bfloat16 [768, 768], replicated, may hold values from -0.21875 to 0.21875
- self_value: bfloat16 [768, 768], replicated, may hold values from -0.21875 to 0.21875
- self_output: bfloat16 [768, 768], replicated, may hold values from -0.4375 to 0.4375
- first_gain: float32 [768], replicated, may hold values from 0.5 to 1.5
- first_bias: float32 [768], replicated, may hold values from -3 to 3
- cross_query: bfloat16 [768, 768], replicated, may hold values from -0.21875 to 0.21875
- cross_key: bfloat16 [768, 768], replicated, may hold values from -0.21875 to 0.21875
- cross_value: bfloat16 [768, 768], replicated, may hold values from -0.21875 to 0.21875
- cross_output: bfloat16 [768, 768], replicated, may hold values from -0.4375 to 0.4375
- second_gain: float32 [768], replicated, may hold values from 0.5 to 1.5
- second_bias: float32 [768], replicated, may hold values from -3 to 3
- expand_weight: bfloat16 [768, 3072], replicated, may hold values from -0.21875 to 0.21875
- reduce_weight: bfloat16 [3072, 768], replicated, may hold values from -0.109375 to 0.109375
- third_gain: float32 [768], replicated, may hold values from 0.5 to 1.5
- third_bias: float32 [768], replicated, may hold values from -3 to 3
- vision_proj: bfloat16 [1024, 768], replicated, may hold values from -0.1875 to 0.1875
Outputs:
- merged: bfloat16 [24576, 768], P(('mod', 'dp'))
- text_grad: float32 [24576, 768], P(('mod', 'dp'))
- patch_grad: float32 [192, 145, 1024], P(('mod', 'dp'))
- grad_self_query: float32 [768, 768], replicated
- grad_self_key: float32 [768, 768], replicated
- grad_self_value: float32 [768, 768], replicated
- grad_self_output: float32 [768, 768], replicated
- grad_first_gain: float32 [768], replicated
- grad_first_bias: float32 [768], replicated
- grad_cross_query: float32 [768, 768], replicated
- grad_cross_key: float32 [768, 768], replicated
- grad_cross_value: float32 [768, 768], replicated
- grad_cross_output: float32 [768, 768], replicated
- grad_second_gain: float32 [768], replicated
- grad_second_bias: float32 [768], replicated
- grad_expand: float32 [768, 3072], replicated
- grad_reduce: float32 [3072, 768], replicated
- grad_third_gain: float32 [768], replicated
- grad_third_bias: float32 [768], replicated
- grad_vision: float32 [1024, 768], replicated
Inputs may be any that keep to these rules, and one draw needn't show every extreme that they name: lengths[b] lists the token counts of the 24 rows packed in order into block b; each row sums to 768. row_image[b, r] is the image, among the 6 images of block (b + 16) mod 32, that row r of block b describes. box_mask[b, r, p] is 1 where row r of block b may attend to patch p of its image; patch 0 is 1 in every row.
All inputs are finite; a program needn't handle non-finite values.
Results may differ from a plain program's by a relative error of at most 0.02.
Values may be sent and summed in bfloat16 or wider, within the bound.
No kernel may reach another device: no remote copies, remote signals or barrier semaphores. Data moves between devices by JAX's collectives and lax.ppermute only.
A program may use at most 384 MiB of HBM per device.

v0:
```python
import jax
import jax.numpy as jnp
from jax import lax
from jax.sharding import PartitionSpec as P

HEADS = 12
HEAD_DIM = 64
TOK_DEV = 768


def from_partner(block, axis, bit):
    count = lax.axis_size(axis)
    route = []
    for low in range(count):
        high = low | 1 << bit
        if high != low and high < count:
            route += [(low, high), (high, low)]
    return lax.ppermute(block, axis, route)


def norm_rows(values, gain_row, shift_row):
    centred = values - jnp.mean(values, axis=-1, keepdims=True)
    spread = jnp.mean(centred * centred, axis=-1, keepdims=True)
    return centred * lax.rsqrt(spread + 1e-05) * gain_row + shift_row


def gelu_exact(values):
    return jax.nn.gelu(values, approximate=False)


def matmul(left, right):
    return jnp.dot(left, right, preferred_element_type=jnp.float32)


def matmul_left_t(left, right):
    return lax.dot_general(
        left, right, (((0,), (0,)), ((), ())), preferred_element_type=jnp.float32
    )


def matmul_right_t(left, right):
    return lax.dot_general(
        left, right, (((1,), (1,)), ((), ())), preferred_element_type=jnp.float32
    )


def split_heads(values):
    return values.reshape(values.shape[0], HEADS, HEAD_DIM)


def head_scores(queries, keys_in, allowed):
    raw_scores = jnp.einsum(
        "qhd,khd->hqk",
        split_heads(queries),
        split_heads(keys_in),
        preferred_element_type=jnp.float32,
    ) * HEAD_DIM ** (-0.5)
    return jnp.where(allowed[None], raw_scores, -1e30)


def attend_forward(queries, keys_in, values_in, allowed):
    scores = head_scores(queries, keys_in, allowed)
    row_top = jnp.max(scores, axis=-1, keepdims=True)
    exp_scores = jnp.exp(scores - row_top)
    row_total = jnp.sum(exp_scores, axis=-1, keepdims=True)
    softmax_out = (exp_scores / row_total).astype(jnp.bfloat16)
    mixed_heads = jnp.einsum(
        "hqk,khd->qhd", softmax_out, split_heads(values_in), preferred_element_type=jnp.float32
    )
    return (mixed_heads.reshape(queries.shape[0], -1), row_top + jnp.log(row_total))


def attend_backward(queries, keys_in, values_in, allowed, log_total, grad_mixed):
    scores = head_scores(queries, keys_in, allowed)
    softmax_out = jnp.exp(scores - log_total)
    grad_heads = split_heads(grad_mixed)
    grad_soft = jnp.einsum(
        "qhd,khd->hqk", grad_heads, split_heads(values_in), preferred_element_type=jnp.float32
    )
    row_inner = jnp.sum(softmax_out * grad_soft, axis=-1, keepdims=True)
    grad_scores = (softmax_out * (grad_soft - row_inner)).astype(jnp.bfloat16)
    grad_queries = jnp.einsum(
        "hqk,khd->qhd", grad_scores, split_heads(keys_in), preferred_element_type=jnp.float32
    ) * HEAD_DIM ** (-0.5)
    grad_keys = jnp.einsum(
        "hqk,qhd->khd", grad_scores, split_heads(queries), preferred_element_type=jnp.float32
    ) * HEAD_DIM ** (-0.5)
    grad_values = jnp.einsum(
        "hqk,qhd->khd",
        softmax_out.astype(jnp.bfloat16),
        grad_heads,
        preferred_element_type=jnp.float32,
    )
    return (
        grad_queries.reshape(queries.shape[0], -1).astype(jnp.bfloat16),
        grad_keys.reshape(keys_in.shape[0], -1).astype(jnp.bfloat16),
        grad_values.reshape(keys_in.shape[0], -1).astype(jnp.bfloat16),
    )


def block_masks(row_lengths, row_images, row_boxes, image_count):
    row_ends = jnp.cumsum(row_lengths)
    position = jnp.arange(TOK_DEV, dtype=jnp.int32)
    row_of = jnp.sum((position[:, None] >= row_ends[None, :]).astype(jnp.int32), axis=1)
    same_row = row_of[:, None] == row_of[None, :]
    choose = (row_of[:, None] == jnp.arange(row_lengths.shape[0], dtype=jnp.int32)[None, :]).astype(
        jnp.int32
    )
    token_image = jnp.sum(choose * row_images[None, :], axis=1)
    token_box = jnp.sum(choose[:, :, None] * row_boxes[None, :, :], axis=1)
    patch_count = row_boxes.shape[1]
    key_image = jnp.arange(image_count * patch_count, dtype=jnp.int32) // patch_count
    cross_allowed = (token_image[:, None] == key_image[None, :]) & (
        jnp.tile(token_box, (1, image_count)) > 0
    )
    return (same_row, cross_allowed)


def pack_flat(partials):
    flat = jnp.concatenate([piece.reshape(-1) for piece in partials])
    return flat


def unpack_flat(flat, partials):
    pieces = []
    offset = 0
    for piece in partials:
        count = piece.size
        pieces.append(flat[offset : offset + count].reshape(piece.shape))
        offset = offset + count
    return tuple(pieces)


def on_device(
    text_tokens,
    patches,
    lengths,
    row_image,
    box_mask,
    cotangent,
    self_query,
    self_key,
    self_value,
    self_output,
    first_gain,
    first_bias,
    cross_query,
    cross_key,
    cross_value,
    cross_output,
    second_gain,
    second_bias,
    expand_weight,
    reduce_weight,
    third_gain,
    third_bias,
    vision_proj,
):
    image_count = patches.shape[0]
    same_row, cross_allowed = block_masks(lengths[0], row_image[0], box_mask[0], image_count)
    flat_patches = patches.reshape(image_count * patches.shape[1], patches.shape[2])
    projected = matmul(flat_patches, vision_proj).astype(jnp.bfloat16)
    own_keys = matmul(projected, cross_key).astype(jnp.bfloat16)
    own_values = matmul(projected, cross_value).astype(jnp.bfloat16)
    far_keys, far_values = from_partner((own_keys, own_values), "mod", 0)
    query_s = matmul(text_tokens, self_query).astype(jnp.bfloat16)
    key_s = matmul(text_tokens, self_key).astype(jnp.bfloat16)
    value_s = matmul(text_tokens, self_value).astype(jnp.bfloat16)
    attended, self_log = attend_forward(query_s, key_s, value_s, same_row)
    attended_b = attended.astype(jnp.bfloat16)
    first_sum = text_tokens.astype(jnp.float32) + matmul(attended_b, self_output)
    normed_one, first_back = jax.vjp(norm_rows, first_sum, first_gain, first_bias)
    normed_one_b = normed_one.astype(jnp.bfloat16)
    query_c = matmul(normed_one_b, cross_query).astype(jnp.bfloat16)
    crossed, cross_log = attend_forward(query_c, far_keys, far_values, cross_allowed)
    crossed_b = crossed.astype(jnp.bfloat16)
    second_sum = normed_one + matmul(crossed_b, cross_output)
    normed_two, second_back = jax.vjp(norm_rows, second_sum, second_gain, second_bias)
    normed_two_b = normed_two.astype(jnp.bfloat16)
    hidden = matmul(normed_two_b, expand_weight)
    activated, gelu_back = jax.vjp(gelu_exact, hidden)
    activated_b = activated.astype(jnp.bfloat16)
    third_sum = normed_two + matmul(activated_b, reduce_weight)
    normed_three, third_back = jax.vjp(norm_rows, third_sum, third_gain, third_bias)
    merged = normed_three.astype(jnp.bfloat16)
    grad_third, grad_third_gain, grad_third_bias = third_back(cotangent.astype(jnp.float32))
    grad_third_b = grad_third.astype(jnp.bfloat16)
    grad_reduce = matmul_left_t(activated_b, grad_third_b)
    grad_active = matmul_right_t(grad_third_b, reduce_weight)
    grad_hidden = gelu_back(grad_active)[0].astype(jnp.bfloat16)
    grad_expand = matmul_left_t(normed_two_b, grad_hidden)
    grad_normed_two = grad_third + matmul_right_t(grad_hidden, expand_weight)
    grad_second, grad_second_gain, grad_second_bias = second_back(grad_normed_two)
    grad_second_b = grad_second.astype(jnp.bfloat16)
    grad_cross_output = matmul_left_t(crossed_b, grad_second_b)
    grad_crossed = matmul_right_t(grad_second_b, cross_output).astype(jnp.bfloat16)
    grad_query_c, grad_far_keys, grad_far_values = attend_backward(
        query_c, far_keys, far_values, cross_allowed, cross_log, grad_crossed
    )
    grad_cross_query = matmul_left_t(normed_one_b, grad_query_c)
    grad_normed_one = grad_second + matmul_right_t(grad_query_c, cross_query)
    grad_first, grad_first_gain, grad_first_bias = first_back(grad_normed_one)
    grad_first_b = grad_first.astype(jnp.bfloat16)
    grad_self_output = matmul_left_t(attended_b, grad_first_b)
    grad_attended = matmul_right_t(grad_first_b, self_output).astype(jnp.bfloat16)
    grad_query_s, grad_key_s, grad_value_s = attend_backward(
        query_s, key_s, value_s, same_row, self_log, grad_attended
    )
    grad_self_query = matmul_left_t(text_tokens, grad_query_s)
    grad_self_key = matmul_left_t(text_tokens, grad_key_s)
    grad_self_value = matmul_left_t(text_tokens, grad_value_s)
    text_grad = (
        grad_first
        + matmul_right_t(grad_query_s, self_query)
        + matmul_right_t(grad_key_s, self_key)
        + matmul_right_t(grad_value_s, self_value)
    )
    back_keys, back_values = from_partner((grad_far_keys, grad_far_values), "mod", 0)
    grad_cross_key = matmul_left_t(projected, back_keys)
    grad_cross_value = matmul_left_t(projected, back_values)
    grad_projected = (
        matmul_right_t(back_keys, cross_key) + matmul_right_t(back_values, cross_value)
    ).astype(jnp.bfloat16)
    grad_vision = matmul_left_t(flat_patches, grad_projected)
    patch_grad = matmul_right_t(grad_projected, vision_proj).reshape(patches.shape)
    partials = (
        grad_self_query,
        grad_self_key,
        grad_self_value,
        grad_self_output,
        grad_first_gain,
        grad_first_bias,
        grad_cross_query,
        grad_cross_key,
        grad_cross_value,
        grad_cross_output,
        grad_second_gain,
        grad_second_bias,
        grad_expand,
        grad_reduce,
        grad_third_gain,
        grad_third_bias,
        grad_vision,
    )
    packed = pack_flat(partials)
    shares = lax.psum_scatter(packed, ("mod", "dp"), scatter_dimension=0, tiled=True)
    totals = lax.all_gather(shares.astype(jnp.bfloat16), ("mod", "dp"), axis=0, tiled=True).astype(
        shares.dtype
    )
    return (merged, text_grad, patch_grad) + unpack_flat(totals, partials)


def solution(mesh):
    placed = (
        P(("mod", "dp"), None),
        P(("mod", "dp"), None, None),
        P(("mod", "dp"), None),
        P(("mod", "dp"), None),
        P(("mod", "dp"), None, None),
        P(("mod", "dp"), None),
        P(),
        P(),
        P(),
        P(),
        P(),
        P(),
        P(),
        P(),
        P(),
        P(),
        P(),
        P(),
        P(),
        P(),
        P(),
        P(),
        P(),
    )
    return jax.shard_map(
        on_device,
        mesh=mesh,
        in_specs=placed,
        out_specs=(
            P(("mod", "dp"), None),
            P(("mod", "dp"), None),
            P(("mod", "dp"), None, None),
            P(),
            P(),
            P(),
            P(),
            P(),
            P(),
            P(),
            P(),
            P(),
            P(),
            P(),
            P(),
            P(),
            P(),
            P(),
            P(),
            P(),
        ),
        check_vma=False,
    )
```

profile of v0, /device:TPU:0, one launch (start us, length us, event | category | flops | bytes accessed | tf_op | source)
XLA Modules:
  0.0 1722.9 jit_solution(7172087861894578238)
XLA Ops:
  33.6 11.7 fusion.63
  45.3 11.6 fusion.1
  56.9 12.1 fusion.34
  81.3 15.0 fusion.12
  96.3 14.0 fusion
  112.8 17.0 fusion.30
  134.0 27.8 %multiply_convert_fusion.2 = (bf16[768,3072]{1,0:T(8,128)(2,1)}, f32[768,3072]{1,0:T(8,128)}, f32[768,3072]{1,0:T(8,128)}) fusion(bf16[768,3072]{1,0:T(8,128)(2,1)S(1)} %bitcast.159, f32[768,768]{0,1:T(8,128)S(1)} %get-tuple-element.143, f32[768]{0:T(1024)S(1)} %copy-done.88, f32[768]{0:T(1024)S(1)} %copy-done.64, f32[768]{0:T(1024)S(1)} %fusion.44, ...), kind=kOutput, calls=%fused_computation.27 | convolution fusion | flops 3780182016 | bytes 30683136 | tf_op jit(solution)/shard_map/dot_general | solution.py:32
  173.3 13.4 add_convert_fusion
  186.7 9.4 multiply_reduce_fusion.3
  199.0 26.0 %multiply_reduce_fusion = (f32[12,768]{1,0:T(8,128)S(1)}, f32[12,768,870]{1,2,0:T(8,128)}) fusion(f32[12,768]{1,0:T(8,128)S(1)} %log_add_fusion.1, f32[12,768,870]{1,2,0:T(8,128)} %get-tuple-element.141, pred[768,870]{0,1:T(8,128)(4,1)S(1)} %compare_and_fusion, bf16[768,12,64]{0,2,1:T(8,128)(2,1)S(1)} %bitcast.142, bf16[870,12,64]{0,2,1:T(8,128)(2,1)S(1)} %bitcast.132), kind=kOutput, calls=%fused_computation.1 | convolution fusion | flops 1066374144 | bytes 67401216 | tf_op jit(solution)/shard_map/qhd,khd->hqk/dot_general | solution.py:77
  225.0 26.5 %multiply_convert_fusion = bf16[12,768,870]{1,2,0:T(8,128)(2,1)} fusion(f32[12,768,870]{1,2,0:T(8,128)} %get-tuple-element.149, f32[12,768]{1,0:T(8,128)S(1)} %get-tuple-element.148, f32[12,768]{1,0:T(8,128)S(1)} %log_add_fusion.1, f32[12,768,870]{1,2,0:T(8,128)} %get-tuple-element.141, pred[768,870]{0,1:T(8,128)(4,1)S(1)} %compare_and_fusion), kind=kLoop, calls=%fused_computation | loop fusion | flops 48107520 | bytes 80921088 | tf_op jit(solution)/shard_map/convert_element_type | solution.py:81
  265.5 23.0 %multiply_reduce_fusion.1 = (f32[12,768]{1,0:T(8,128)}, f32[12,768,768]{1,2,0:T(8,128)}) fusion(f32[12,768,768]{1,2,0:T(8,128)} %get-tuple-element.137, f32[12,768]{1,0:T(8,128)S(1)} %copy-done.44, bf16[768,12,64]{0,2,1:T(8,128)(2,1)S(1)} %bitcast.140, bf16[768,12,64]{0,2,1:T(8,128)(2,1)} %bitcast.152), kind=kOutput, calls=%fused_computation.8 | convolution fusion | flops 927194112 | bytes 59056128 | tf_op jit(solution)/shard_map/qhd,khd->hqk/dot_general | solution.py:77
  288.5 23.3 %multiply_convert_fusion.1 = bf16[12,768,768]{1,2,0:T(8,128)(2,1)} fusion(f32[12,768,768]{1,2,0:T(8,128)} %get-tuple-element.152, f32[12,768,768]{1,2,0:T(8,128)} %get-tuple-element.137, f32[12,768]{1,0:T(8,128)} %get-tuple-element.151, f32[12,768]{1,0:T(8,128)S(1)} %copy-done.44), kind=kLoop, calls=%fused_computation.7 | loop fusion | flops 28311552 | bytes 70852608 | tf_op jit(solution)/shard_map/convert_element_type | solution.py:81
  311.9 10.5 multiply_convert_fusion.4
  331.1 12.6 fusion.31
  343.7 16.2 fusion.27
  359.9 11.3 multiply_convert_fusion.3
  447.5 9.8 copy.135
  464.7 10.7 reshape.485
  478.1 21.3 %dynamic-update-slice.7 = f32[10228224]{0:T(1024)} dynamic-update-slice(f32[10228224]{0:T(1024)} %constant_dynamic-update-slice_fusion.6, f32[589824]{0:T(1024)} %reshape.480, s32[]{} %constant.125) | dynamic-update-slice | bytes 4718596
  532.3 21.3 %dynamic-update-slice.8 = f32[10228224]{0:T(1024)} dynamic-update-slice(f32[10228224]{0:T(1024)} %dynamic-update-slice.7, f32[589824]{0:T(1024)} %reshape.481, s32[]{} %constant.126) | dynamic-update-slice | bytes 4718596
  553.6 21.3 %dynamic-update-slice.9 = f32[10228224]{0:T(1024)} dynamic-update-slice(f32[10228224]{0:T(1024)} %dynamic-update-slice.8, f32[589824]{0:T(1024)} %reshape.482, s32[]{} %constant.127) | dynamic-update-slice | bytes 4718596
  574.9 21.3 %dynamic-update-slice.10 = f32[10228224]{0:T(1024)} dynamic-update-slice(f32[10228224]{0:T(1024)} %dynamic-update-slice.9, f32[589824]{0:T(1024)} %reshape.483, s32[]{} %constant.128) | dynamic-update-slice | bytes 4718596
  598.8 9.2 constant_dynamic-update-slice_fusion.3
  614.6 27.5 %dynamic-update-slice.17 = f32[10228224]{0:T(1024)} dynamic-update-slice(f32[10228224]{0:T(1024)} %constant_dynamic-update-slice_fusion, f32[786432]{0:T(1024)} %reshape.486, s32[]{} %constant.135) | dynamic-update-slice | bytes 6291460 | tf_op jit(solution)/shard_map/concatenate | solution.py:120
  642.1 653.9 %all-reduce.6 = bf16[10228224]{0:T(1024)(128)(2,1)} all-reduce(f32[10228224]{0:T(1024)} %dynamic-update-slice.17), channel_id=2, replica_groups=mesh['mod'=2,'dp'=16] {'mod','dp'}, use_global_device_ids=true, to_apply=%region_28.29.clone | all-reduce | flops 10228224 | bytes 61369344
  1304.3 10.5 dynamic-update-slice
  1337.0 301.4 %all-reduce.5.cloned.1.call-done = bf16[10228224]{0:T(1024)(128)(2,1)} async-done(((bf16[10228224]{0:T(1024)(128)(2,1)}), bf16[10228224]{0:T(1024)(128)(2,1)}) %all-reduce.5.cloned.1.call-update) | async-done | bytes 20456464
  1638.4 9.2 fusion.62
  1674.4 9.6 fusion.61
  1684.0 10.9 reshape.487
  1694.9 11.3 slice.173
  (336 shorter events, 276.6 us)
Async XLA Ops:
  7.2 1631.2 %all-reduce.5.cloned.1.call-start = ((), (), s32[]{:S(2)}) async-start(), calls=%async_computation | async-start | bytes 40914944
  13.6 96.7 %collective-permute-start = (bf16[870,768]{1,0:T(8,128)(2,1)}, bf16[870,768]{1,0:T(8,128)(2,1)}, u32[]{:S(2)}, u32[]{:S(2)}) collective-permute-start(bf16[870,768]{1,0:T(8,128)(2,1)} %convolution_convert_fusion.1), channel_id=1, source_target_pairs={{0,16},{16,0},{1,17},{17,1},{2,18},{18,2},{3,19},{19,3},{4,20},{20... | collective-permute-start | bytes 4008968 | tf_op jit(solution)/shard_map/ppermute | solution.py:18
  18.9 59.5 %collective-permute-start.1 = (bf16[870,768]{1,0:T(8,128)(2,1)}, bf16[870,768]{1,0:T(8,128)(2,1)}, u32[]{:S(2)}, u32[]{:S(2)}) collective-permute-start(bf16[870,768]{1,0:T(8,128)(2,1)} %convolution_convert_fusion), channel_id=1, source_target_pairs={{0,16},{16,0},{1,17},{17,1},{2,18},{18,2},{3,19},{19,3},{4,20},{20... | collective-permute-start | bytes 4008968 | tf_op jit(solution)/shard_map/ppermute | solution.py:18
  30.7 26.2 %copy-start.43 = (bf16[768,768]{0,1:T(8,128)(2,1)}, bf16[768,768]{0,1:T(8,128)(2,1)S(1)}, u32[]{:S(2)}) copy-start(bf16[768,768]{0,1:T(8,128)(2,1)S(1)} %convolution_convert_fusion.8) | copy-start | bytes 3538948
  33.6 11.7 copy-start.1
  56.9 12.2 copy-start.41
  56.9 12.2 copy-start.77
  71.7 58.1 %copy-start.45 = (f32[768]{0:T(1024)}, f32[768]{0:T(1024)S(1)}, u32[]{:S(2)}) copy-start(f32[768]{0:T(1024)S(1)} %broadcast_multiply_fusion.2) | copy-start | bytes 9220
  74.5 55.4 %copy-start.52 = (f32[768]{0:T(1024)}, f32[768]{0:T(1024)S(1)}, u32[]{:S(2)}) copy-start(f32[768]{0:T(1024)S(1)} %fusion.43) | copy-start | bytes 9220
  78.4 17.9 %copy-start.20 = (bf16[768,768]{0,1:T(8,128)(2,1)}, bf16[768,768]{0,1:T(8,128)(2,1)S(1)}, u32[]{:S(2)}) copy-start(bf16[768,768]{0,1:T(8,128)(2,1)S(1)} %convolution_convert_fusion.5) | copy-start | bytes 3538948
  112.8 17.0 copy-start.9
  129.9 31.9 %slice-start.3 = ((s8[4718592]{0:T(1024)(128)(4,1)}), s8[4194304]{0:T(1024)(128)(4,1)S(1)}, s32[]{:S(2)}) async-start(s8[4718592]{0:T(1024)(128)(4,1)} %bitcast.156), calls=%async_computation.4 | async-start | bytes 8388608
  133.1 63.1 %copy-start.12 = (f32[768,768]{0,1:T(8,128)}, f32[768,768]{0,1:T(8,128)S(1)}, u32[]{:S(2)}) copy-start(f32[768,768]{0,1:T(8,128)S(1)} %get-tuple-element.143) | copy-start | bytes 7077892
  134.0 27.8 %slice-start.4 = ((s8[4718592]{0:T(1024)(128)(4,1)}), s8[524288]{0:T(1024)(128)(4,1)S(1)}, s32[]{:S(2)}) async-start(s8[4718592]{0:T(1024)(128)(4,1)} %bitcast.156), calls=%async_computation.5 | async-start | bytes 1048576
  168.9 17.9 %copy-start.16 = (f32[768,768]{0,1:T(8,128)}, f32[768,768]{0,1:T(8,128)S(1)}, u32[]{:S(2)}) copy-start(f32[768,768]{0,1:T(8,128)S(1)} %get-tuple-element.146) | copy-start | bytes 7077892
  168.9 17.8 %copy-start.49 = (f32[768]{0:T(1024)}, f32[768]{0:T(1024)S(1)}, u32[]{:S(2)}) copy-start(f32[768]{0:T(1024)S(1)} %broadcast_multiply_fusion) | copy-start | bytes 9220
  170.4 16.3 copy-start.56
  170.4 16.3 copy-start.58
  173.3 13.5 copy-start.67
  196.9 63.8 %copy-start.70 = (f32[768]{0:T(1024)}, f32[768]{0:T(1024)S(1)}, u32[]{:S(2)}) copy-start(f32[768]{0:T(1024)S(1)} %negate_multiply_fusion.2) | copy-start | bytes 9220
  198.6 26.4 %copy-start.28 = (bf16[768,768]{0,1:T(8,128)(2,1)}, bf16[768,768]{0,1:T(8,128)(2,1)S(1)}, u32[]{:S(2)}) copy-start(bf16[768,768]{0,1:T(8,128)(2,1)S(1)} %convolution_convert_fusion.4) | copy-start | bytes 3538948
  265.5 23.0 %copy-start.26 = (bf16[768,768]{0,1:T(8,128)(2,1)}, bf16[768,768]{0,1:T(8,128)(2,1)S(1)}, u32[]{:S(2)}) copy-start(bf16[768,768]{0,1:T(8,128)(2,1)S(1)} %convolution_convert_fusion.3) | copy-start | bytes 3538948
  288.5 23.3 %copy-start.7 = (bf16[768,768]{0,1:T(8,128)(2,1)S(1)}, bf16[768,768]{0,1:T(8,128)(2,1)}, u32[]{:S(2)}) copy-start(bf16[768,768]{0,1:T(8,128)(2,1)} %copy-done.6) | copy-start | bytes 3538948
  343.7 16.2 copy-start.21
  390.0 116.8 %collective-permute-start.3 = (bf16[870,768]{1,0:T(8,128)(2,1)}, bf16[870,768]{1,0:T(8,128)(2,1)}, u32[]{:S(2)}, u32[]{:S(2)}) collective-permute-start(bf16[870,768]{1,0:T(8,128)(2,1)} %copy.119), channel_id=1, source_target_pairs={{0,16},{16,0},{1,17},{17,1},{2,18},{18,2},{3,19},{19,3},{4,20},{20... | collective-permute-start | bytes 4008968 | tf_op jit(solution)/shard_map/ppermute | solution.py:18
  393.6 105.9 %collective-permute-start.2 = (bf16[870,768]{1,0:T(8,128)(2,1)}, bf16[870,768]{1,0:T(8,128)(2,1)}, u32[]{:S(2)}, u32[]{:S(2)}) collective-permute-start(bf16[870,768]{1,0:T(8,128)(2,1)} %copy.118), channel_id=1, source_target_pairs={{0,16},{16,0},{1,17},{17,1},{2,18},{18,2},{3,19},{19,3},{4,20},{20... | collective-permute-start | bytes 4008968 | tf_op jit(solution)/shard_map/ppermute | solution.py:18
  444.1 13.2 slice-start.7
  464.7 10.7 copy-start.69
  478.1 21.4 %copy-start.95 = (bf16[870,768]{1,0:T(8,128)(2,1)S(1)}, bf16[870,768]{1,0:T(8,128)(2,1)}, u32[]{:S(2)}) copy-start(bf16[870,768]{1,0:T(8,128)(2,1)} %copy-done.94) | copy-start | bytes 4008964
  574.9 21.3 %copy-start.66 = (f32[768]{0:T(1024)S(1)}, f32[768]{0:T(1024)}, u32[]{:S(2)}) copy-start(f32[768]{0:T(1024)} %get-tuple-element.100) | copy-start | bytes 9220
  574.9 22.6 %copy-start.65 = (f32[768]{0:T(1024)S(1)}, f32[768]{0:T(1024)}, u32[]{:S(2)}) copy-start(f32[768]{0:T(1024)} %get-tuple-element.108) | copy-start | bytes 9220
  574.9 33.2 %slice-start = ((s8[9437184]{0:T(1024)(128)(4,1)}), s8[1048576]{0:T(1024)(128)(4,1)S(1)}, s32[]{:S(2)}) async-start(s8[9437184]{0:T(1024)(128)(4,1)} %bitcast.125), calls=%async_computation.1 | async-start | bytes 2097152
  (78 other events, 355.7 us)
Sparse Core Ops, SparseCore 0:
  1314.9 323.3 all-reduce.4
where the time goes:
time: 1740 us; the launch traced here: 1720 us
  blocking collectives  654 us (38%)
  local copies, waits for them, and re-layouts  339 us (19%)
  matrix products  320 us (18%)
  waiting for transfers between devices  301 us (17%)
  other arithmetic  88.5 us (5%)
    unnamed x1, blocking collectives  654 us
    unnamed x2, waiting for transfers between devices  301 us
    unnamed x234, local copies, waits for them, and re-layouts  163 us
    slice x14, local copies, waits for them, and re-layouts, unpack_flat(): pieces.append(flat[offset:offset + count].reshape(piece.shape))  66.3 us
    dot_general x11, matrix products, matmul(): return jnp.dot(left, right, preferred_element_type=jnp.float32)  54.6 us
    convert_element_type x2, other arithmetic, attend_backward(): grad_scores = (softmax_out * (grad_soft - row_inner)).astype(jnp.bfloat16)  49.8 us
    dot_general x2, matrix products, attend_backward(): jnp.einsum('qhd,khd->hqk', grad_heads, split_heads(values_in), preferred_...  49 us
    dot_general x11, matrix products, matmul_left_t(): lax.dot_general(left, right, (((0,), (0,)), ((), ())), preferred_element_...  48.4 us
  transfers between devices with their start and end apart: 5, of which 1 were waited for; matrix products, arithmetic and copies ran while one was open for 13% of the time, Pallas kernels for 0%

commit v1 on v0

--- a/solution.py
+++ b/solution.py
@@ -116,19 +116,66 @@
     return (same_row, cross_allowed)
 
 
-def pack_flat(partials):
-    flat = jnp.concatenate([piece.reshape(-1) for piece in partials])
-    return flat
-
-
-def unpack_flat(flat, partials):
-    pieces = []
-    offset = 0
-    for piece in partials:
-        count = piece.size
-        pieces.append(flat[offset : offset + count].reshape(piece.shape))
-        offset = offset + count
-    return tuple(pieces)
+def flip_bit(values, axis, bit):
+    count = lax.axis_size(axis)
+    return lax.ppermute(values, axis, [(i, i ^ (1 << bit)) for i in range(count)])
+
+
+def my_bit(axis, bit):
+    return (lax.axis_index(axis) >> bit) & 1
+
+
+def stage_orders():
+    dp_bits = lax.axis_size("dp").bit_length() - 1
+    mod_bits = lax.axis_size("mod").bit_length() - 1
+    core = [("dp", 0)]
+    near = [("dp", 1)]
+    across = [("mod", bit) for bit in range(mod_bits)]
+    rest = [("dp", bit) for bit in range(2, dp_bits)]
+    return (core + near + across + rest, core + across + near + rest)
+
+
+def halves(values, dim):
+    shape = values.shape
+    return values.reshape(shape[:dim] + (2, shape[dim] // 2) + shape[dim + 1 :])
+
+
+def sum_scatter(values, order):
+    for step, (axis, bit) in enumerate(order):
+        if step >= 5:
+            values = values + flip_bit(values, axis, bit)
+            continue
+        dim = 0 if values.shape[0] % 32 == 0 else 1
+        pair = halves(values, dim)
+        mine = my_bit(axis, bit)
+        away = lax.dynamic_index_in_dim(pair, 1 - mine, dim, False)
+        keep = lax.dynamic_index_in_dim(pair, mine, dim, False)
+        values = keep + flip_bit(away, axis, bit)
+    return values
+
+
+def gather_back(values, order, shape):
+    dims = []
+    rows, columns = shape
+    for step in range(min(5, len(order))):
+        dim = 0 if rows % 32 == 0 else 1
+        rows, columns = (rows // 2, columns) if dim == 0 else (rows, columns // 2)
+        dims.append(dim)
+    for step in reversed(range(len(dims))):
+        axis, bit = order[step]
+        other = flip_bit(values, axis, bit)
+        low = my_bit(axis, bit) == 0
+        if step == 0:
+            values, other = values.astype(jnp.float32), other.astype(jnp.float32)
+        values = jnp.concatenate(
+            [jnp.where(low, values, other), jnp.where(low, other, values)], axis=dims[step]
+        )
+    return values
+
+
+def total(values, order):
+    values = values.astype(jnp.bfloat16)
+    return gather_back(sum_scatter(values, order), order, values.shape)
 
 
 def on_device(
@@ -223,31 +270,61 @@
     ).astype(jnp.bfloat16)
     grad_vision = matmul_left_t(flat_patches, grad_projected)
     patch_grad = matmul_right_t(grad_projected, vision_proj).reshape(patches.shape)
-    partials = (
-        grad_self_query,
-        grad_self_key,
-        grad_self_value,
-        grad_self_output,
-        grad_first_gain,
-        grad_first_bias,
-        grad_cross_query,
-        grad_cross_key,
-        grad_cross_value,
-        grad_cross_output,
-        grad_second_gain,
-        grad_second_bias,
-        grad_expand,
-        grad_reduce,
-        grad_third_gain,
-        grad_third_bias,
-        grad_vision,
-    )
-    packed = pack_flat(partials)
-    shares = lax.psum_scatter(packed, ("mod", "dp"), scatter_dimension=0, tiled=True)
-    totals = lax.all_gather(shares.astype(jnp.bfloat16), ("mod", "dp"), axis=0, tiled=True).astype(
-        shares.dtype
-    )
-    return (merged, text_grad, patch_grad) + unpack_flat(totals, partials)
+    one_way, other_way = stage_orders()
+    half_ff = grad_reduce.shape[0] // 2
+    sum_reduce = jnp.concatenate(
+        [total(grad_reduce[:half_ff], one_way), total(grad_reduce[half_ff:], other_way)], axis=0
+    )
+    sum_expand = jnp.concatenate(
+        [total(grad_expand[:, :half_ff], one_way), total(grad_expand[:, half_ff:], other_way)],
+        axis=1,
+    )
+    width = grad_cross_query.shape[1]
+
+    def couple(left, right, order):
+        both = total(jnp.concatenate([left, right], axis=1), order)
+        return both[:, :width], both[:, width:]
+
+    sum_cross_output, sum_cross_query = couple(grad_cross_output, grad_cross_query, one_way)
+    sum_cross_key, sum_cross_value = couple(grad_cross_key, grad_cross_value, other_way)
+    sum_vision = total(grad_vision, one_way)
+    sum_self_output, sum_self_query = couple(grad_self_output, grad_self_query, other_way)
+    sum_self_key, sum_self_value = couple(grad_self_key, grad_self_value, one_way)
+    small = lax.psum(
+        jnp.stack(
+            [
+                grad_first_gain,
+                grad_first_bias,
+                grad_second_gain,
+                grad_second_bias,
+                grad_third_gain,
+                grad_third_bias,
+            ]
+        ),
+        ("mod", "dp"),
+    )
+    return (
+        merged,
+        text_grad,
+        patch_grad,
+        sum_self_query,
+        sum_self_key,
+        sum_self_value,
+        sum_self_output,
+        small[0],
+        small[1],
+        sum_cross_query,
+        sum_cross_key,
+        sum_cross_value,
+        sum_cross_output,
+        small[2],
+        small[3],
+        sum_expand,
+        sum_reduce,
+        small[4],
+        small[5],
+        sum_vision,
+    )
 
 
 def solution(mesh):

time: 1740 us -> 881 us (0.51)
  blocking collectives: 654 us -> 77.6 us
  local copies, waits for them, and re-layouts: 339 us -> 68.9 us
  waiting for transfers between devices: 301 us -> 154 us
  starting transfers between devices: 5.04 us -> 91.9 us
  other arithmetic: 88.5 us -> 171 us
    unnamed x1 -> x0, blocking collectives: 654 us -> none
    unnamed x2 -> x0, waiting for transfers between devices: 301 us -> none
    ppermute x0 -> x90, waiting for transfers between devices: none -> 154 us  [flip_bit(): return lax.ppermute(values, axis, [(i, i ^ 1 << bit) for i in range(count)])]
    unnamed x234 -> x316, local copies, waits for them, and re-layouts: 163 us -> 25.2 us
    ppermute x0 -> x90, starting transfers between devices: none -> 86.8 us  [flip_bit(): return lax.ppermute(values, axis, [(i, i ^ 1 << bit) for i in range(count)])]
    psum x0 -> x1, blocking collectives: none -> 77.6 us  [on_device(): lax.psum(jnp.stack([grad_first_gain, grad_first_bias, grad_second_gain, g...]
    slice x14 -> x3, local copies, waits for them, and re-layouts: 66.3 us -> 3.83 us  [the longest x1 2.83 us: on_device(): grad_reduce[:half_ff]]
    reshape x11 -> x13, local copies, waits for them, and re-layouts: 52 us -> 4.39 us  [the longest x7 4.37 us: halves(): return values.reshape(shape[:dim] + (2, shape[dim] // 2) + shape[dim + 1:])]
  transfers between devices with their start and end apart: 5 -> 94, of which waited for: 1 -> 40; matrix products, arithmetic and copies ran while one was open for 13% -> 28% of each run, Pallas kernels for 0% -> 0%
where the time goes in v1:
time: 881 us; the launch traced here: 875 us
  matrix products  307 us (35%)
  other arithmetic  171 us (19%)
  waiting for transfers between devices  154 us (17%)
  starting transfers between devices  91.9 us (10%)
  blocking collectives  77.6 us (9%)
  local copies, waits for them, and re-layouts  68.9 us (8%)
    ppermute x90, waiting for transfers between devices, flip_bit(): return lax.ppermute(values, axis, [(i, i ^ 1 << bit) for i in range(count)])  154 us
    ppermute x90, starting transfers between devices, flip_bit(): return lax.ppermute(values, axis, [(i, i ^ 1 << bit) for i in range(count)])  86.8 us
    psum x1, blocking collectives, on_device(): lax.psum(jnp.stack([grad_first_gain, grad_first_bias, grad_second_gain, g...  77.6 us
    dot_general x11, matrix products, matmul(): return jnp.dot(left, right, preferred_element_type=jnp.float32)  53.4 us
    convert_element_type x2, other arithmetic, attend_backward(): grad_scores = (softmax_out * (grad_soft - row_inner)).astype(jnp.bfloat16)  49.9 us
    dot_general x2, matrix products, attend_backward(): jnp.einsum('qhd,khd->hqk', grad_heads, split_heads(values_in), preferred_...  48.8 us
    dot_general x11, matrix products, matmul_right_t(): lax.dot_general(left, right, (((1,), (1,)), ((), ())), preferred_element_...  42.6 us
    dot_general x11, matrix products, matmul_left_t(): lax.dot_general(left, right, (((0,), (0,)), ((), ())), preferred_element_...  40 us
  transfers between devices with their start and end apart: 94, of which 40 were waited for; matrix products, arithmetic and copies ran while one was open for 28% of the time, Pallas kernels for 0%

profile of v1, /device:TPU:0, one launch (start us, length us, event | category | flops | bytes accessed | tf_op | source)
XLA Modules:
  0.0 875.3 jit_solution(12860445780892064627)
XLA Ops:
  20.3 11.8 %fusion.83 = (f32[12,768]{1,0:T(8,128)S(1)}, f32[12,768,768]{1,2,0:T(8,128)}) fusion(bf16[768,12,64]{0,2,1:T(8,128)(2,1)S(1)} %bitcast.382, bf16[768,12,64]{0,2,1:T(8,128)(2,1)S(1)} %bitcast.378, pred[768,768]{0,1:T(8,128)(4,1)S(1)} %broadcast_compare_fusion), kind=kOutput, calls=%fused_computation.428 | convolution fusion | flops 927194112 | bytes 31297536 | tf_op jit(solution)/shard_map/qhd,khd->hqk/dot_general | solution.py:52
  32.1 11.6 %fusion.1 = f32[12,768]{1,0:T(8,128)S(1)} fusion(f32[12,768,768]{1,2,0:T(8,128)} %get-tuple-element.261, f32[12,768]{1,0:T(8,128)S(1)} %get-tuple-element.260), kind=kLoop, calls=%fused_computation.13 | loop fusion | flops 14146560 | bytes 28385280 | tf_op jit(solution)/shard_map/reduce_sum | solution.py:65
  43.7 11.9 %fusion.38 = bf16[12,64,768]{2,1,0:T(8,128)(2,1)S(1)} fusion(bf16[768,12,64]{0,2,1:T(8,128)(2,1)S(1)} %bitcast.475, f32[12,768,768]{1,2,0:T(8,128)} %get-tuple-element.261, f32[12,768]{1,0:T(8,128)S(1)} %fusion.1, f32[12,768]{1,0:T(8,128)S(1)} %get-tuple-element.260), kind=kOutput, calls=%fused_computation.154 | convolution fusion | flops 927793152 | bytes 30744576 | tf_op jit(solution)/shard_map/hqk,khd->qhd/dot_general | solution.py:67
  76.8 15.2 %fusion.12 = (f32[12,768]{1,0:T(8,128)S(1)}, f32[12,768,870]{1,2,0:T(8,128)}) fusion(pred[768,870]{0,1:T(8,128)(4,1)S(1)} %compare_and_fusion, bf16[768,12,64]{0,2,1:T(8,128)(2,1)} %bitcast.392, bf16[870,12,64]{0,2,1:T(8,128)(2,1)} %bitcast.376), kind=kOutput, calls=%fused_computation.23 | convolution fusion | flops 1050338304 | bytes 35292672 | tf_op jit(solution)/shard_map/qhd,khd->hqk/dot_general | solution.py:52
  92.0 14.0 %fusion = f32[12,768]{1,0:T(8,128)S(1)} fusion(f32[12,768]{1,0:T(8,128)S(1)} %get-tuple-element.264, f32[12,768,870]{1,2,0:T(8,128)} %get-tuple-element.265, pred[768,870]{0,1:T(8,128)(4,1)S(1)} %compare_and_fusion), kind=kLoop, calls=%fused_computation.6 | loop fusion | flops 32062464 | bytes 32813568 | tf_op jit(solution)/shard_map/reduce_sum | solution.py:65
  109.2 16.6 %fusion.34 = bf16[12,64,768]{2,1,0:T(8,128)(2,1)} fusion(bf16[870,12,64]{0,2,1:T(8,128)(2,1)} %bitcast.380, f32[12,768]{1,0:T(8,128)} %copy-done.107, f32[12,768]{1,0:T(8,128)S(1)} %get-tuple-element.264, f32[12,768,870]{1,2,0:T(8,128)} %get-tuple-element.265, pred[768,870]{0,1:T(8,128)(4,1)S(1)} %compare_and_fusion), kind=kOutput, calls=%fused_computation.138 | convolution fusion | flops 1066973184 | bytes 35329536 | tf_op jit(solution)/shard_map/hqk,khd->qhd/dot_general | solution.py:67
  129.9 27.6 %multiply_convert_fusion.2 = (bf16[768,3072]{1,0:T(8,128)(2,1)}, f32[768,3072]{1,0:T(8,128)}, f32[768,3072]{1,0:T(8,128)}) fusion(bf16[768,3072]{1,0:T(8,128)(2,1)S(1)} %bitcast.496, f32[768,768]{0,1:T(8,128)S(1)} %get-tuple-element.267, f32[768]{0:T(1024)S(1)} %copy-done.141, f32[768]{0:T(1024)S(1)} %copy-done.121, f32[768]{0:T(1024)S(1)} %fusion.68, ...), kind=kOutput, calls=%fused_computation.29 | convolution fusion | flops 3780182016 | bytes 30683136 | tf_op jit(solution)/shard_map/dot_general | solution.py:32
  157.5 6.9 fusion.86
  168.8 13.4 %add_convert_fusion = bf16[768,3072]{1,0:T(8,128)(2,1)} fusion(f32[768,3072]{1,0:T(8,128)} %get-tuple-element.142, f32[768,3072]{1,0:T(8,128)} %get-tuple-element.268, bf16[3072,768]{1,0:T(8,128)(2,1)} %param.42, f32[768]{0:T(1024)S(1)} %negate_multiply_fusion.3, bf16[768,768]{0,1:T(8,128)(2,1)S(1)} %copy.135, f32[768,768]{0,1:T(8,128)S(1)} %get-tuple-element.270, ...), kind=kOutput, calls=%fused_computation.28 | convolution fusion | flops 3662217216 | bytes 31865856 | tf_op jit(solution)/shard_map/dot_general | solution.py:42
  182.2 9.4 %multiply_reduce_fusion.3 = (f32[768]{0:T(1024)}, f32[768]{0:T(1024)S(1)}, f32[768]{0:T(1024)}, f32[768,768]{0,1:T(8,128)S(1)}) fusion(f32[768,768]{0,1:T(8,128)S(1)} %get-tuple-element.267, f32[768]{0:T(1024)S(1)} %fusion.68, f32[768]{0:T(1024)S(1)} %broadcast_multiply_fusion.1, f32[768]{0:T(1024)S(1)} %copy-done.121, ...), kind=kOutput, calls=%fused_computation.107 | convolution fusion | flops 3633903360 | bytes 17728512 | tf_op jit(solution)/shard_map/dot_general | solution.py:42
  195.0 15.8 %fusion.31 = bf16[12,64,870]{2,1,0:T(8,128)(2,1)} fusion(bf16[768,12,64]{0,2,1:T(8,128)(2,1)} %bitcast.429, f32[12,768]{1,0:T(8,128)S(1)} %log_add_fusion.1, f32[12,768,870]{1,2,0:T(8,128)} %get-tuple-element.265, pred[768,870]{0,1:T(8,128)(4,1)S(1)} %compare_and_fusion), kind=kOutput, calls=%fused_computation.134 | convolution fusion | flops 1059033600 | bytes 35292672 | tf_op jit(solution)/shard_map/hqk,qhd->khd/dot_general | solution.py:88
  210.8 26.6 %multiply_reduce_fusion = (f32[12,768]{1,0:T(8,128)S(1)}, f32[12,768,870]{1,2,0:T(8,128)}) fusion(f32[12,768]{1,0:T(8,128)S(1)} %log_add_fusion.1, f32[12,768,870]{1,2,0:T(8,128)} %get-tuple-element.265, pred[768,870]{0,1:T(8,128)(4,1)S(1)} %compare_and_fusion, bf16[768,12,64]{0,2,1:T(8,128)(2,1)} %bitcast.430, bf16[870,12,64]{0,2,1:T(8,128)(2,1)} %bitcast.381), kind=kOutput, calls=%fused_computation.1 | convolution fusion | flops 1066374144 | bytes 67401216 | tf_op jit(solution)/shard_map/qhd,khd->hqk/dot_general | solution.py:77
  237.5 8.7 convolution_convert_fusion
  246.2 8.3 convolution_convert_fusion.1
  254.5 26.5 %multiply_convert_fusion = bf16[12,768,870]{1,2,0:T(8,128)(2,1)} fusion(f32[12,768,870]{1,2,0:T(8,128)} %get-tuple-element.273, f32[12,768]{1,0:T(8,128)S(1)} %get-tuple-element.272, f32[12,768]{1,0:T(8,128)S(1)} %log_add_fusion.1, f32[12,768,870]{1,2,0:T(8,128)} %get-tuple-element.265, pred[768,870]{0,1:T(8,128)(4,1)S(1)} %compare_and_fusion), kind=kLoop, calls=%fused_computation | loop fusion | flops 48107520 | bytes 80921088 | tf_op jit(solution)/shard_map/convert_element_type | solution.py:81
  281.0 11.7 %multiply_convert_fusion.3 = bf16[12,64,870]{2,1,0:T(8,128)(2,1)} fusion(bf16[768,12,64]{0,2,1:T(8,128)(2,1)} %bitcast.393, bf16[12,768,870]{1,2,0:T(8,128)(2,1)} %multiply_convert_fusion), kind=kOutput, calls=%fused_computation.78 | convolution fusion | flops 1027630080 | bytes 18551808 | tf_op jit(solution)/shard_map/hqk,qhd->khd/dot_general | solution.py:85
  292.8 8.7 multiply_convert_fusion.6
  305.8 22.2 %multiply_reduce_fusion.1 = (f32[12,768]{1,0:T(8,128)S(1)}, f32[12,768,768]{1,2,0:T(8,128)}) fusion(f32[12,768,768]{1,2,0:T(8,128)} %get-tuple-element.261, f32[12,768]{1,0:T(8,128)S(1)} %copy-done.104, bf16[768,12,64]{0,2,1:T(8,128)(2,1)S(1)} %bitcast.427, bf16[768,12,64]{0,2,1:T(8,128)(2,1)} %bitcast.476), kind=kOutput, calls=%fused_computation.8 | convolution fusion | flops 927194112 | bytes 59056128 | tf_op jit(solution)/shard_map/qhd,khd->hqk/dot_general | solution.py:77
  328.0 12.6 %fusion.35 = bf16[12,64,768]{2,1,0:T(8,128)(2,1)} fusion(bf16[768,12,64]{0,2,1:T(8,128)(2,1)S(1)} %bitcast.428, f32[12,768,768]{1,2,0:T(8,128)} %get-tuple-element.261, f32[12,768]{1,0:T(8,128)S(1)} %copy-done.104), kind=kOutput, calls=%fused_computation.153 | convolution fusion | flops 920715264 | bytes 30707712 | tf_op jit(solution)/shard_map/hqk,qhd->khd/dot_general | solution.py:88
  340.6 23.4 %multiply_convert_fusion.1 = bf16[12,768,768]{1,2,0:T(8,128)(2,1)} fusion(f32[12,768,768]{1,2,0:T(8,128)} %get-tuple-element.276, f32[12,768,768]{1,2,0:T(8,128)} %get-tuple-element.261, f32[12,768]{1,0:T(8,128)S(1)} %get-tuple-element.275, f32[12,768]{1,0:T(8,128)S(1)} %copy-done.104), kind=kLoop, calls=%fused_computation.7 | loop fusion | flops 28311552 | bytes 70852608 | tf_op jit(solution)/shard_map/convert_element_type | solution.py:81
  364.0 7.7 multiply_convert_fusion.5
  371.7 10.5 %multiply_convert_fusion.4 = bf16[12,64,768]{2,1,0:T(8,128)(2,1)} fusion(bf16[768,12,64]{0,2,1:T(8,128)(2,1)S(1)} %bitcast.383, bf16[12,768,768]{1,2,0:T(8,128)(2,1)} %multiply_convert_fusion.1), kind=kOutput, calls=%fused_computation.110 | convolution fusion | flops 907149312 | bytes 16515072 | tf_op jit(solution)/shard_map/hqk,qhd->khd/dot_general | solution.py:85
  406.4 77.6 %psum.7 = f32[6,768]{1,0:T(8,128)S(1)} all-reduce(f32[6,768]{1,0:T(8,128)S(1)} %stack.2), channel_id=1, replica_groups=mesh['mod'=2,'dp'=16] {'mod','dp'}, use_global_device_ids=true, to_apply=%region_28.29 | all-reduce | flops 4608 | bytes 36864 | tf_op jit(solution)/shard_map/psum | solution.py:293
  576.1 6.8 collective-permute-done.46
  629.2 6.3 collective-permute-done.58
  687.6 8.0 collective-permute-done.86
  726.5 16.0 %collective-permute-done.91 = bf16[128,768]{1,0:T(8,128)(2,1)S(1)} collective-permute-done((bf16[128,768]{1,0:T(8,128)(2,1)S(1)}, bf16[128,768]{1,0:T(8,128)(2,1)S(1)}, u32[]{:S(2)}, u32[]{:S(2)}) %collective-permute-start.91) | collective-permute-done | bytes 196640 | tf_op jit(solution)/shard_map/ppermute | solution.py:121
  778.4 5.7 collective-permute-done.28
  784.1 5.9 collective-permute-done.39
  795.5 6.6 collective-permute-done.40
  814.5 6.1 collective-permute-done.31
  849.2 8.6 maximum_maximum_fusion
  (757 shorter events, 402.7 us)
Async XLA Ops:
  7.1 67.3 %collective-permute-start.1 = (bf16[870,768]{1,0:T(8,128)(2,1)}, bf16[870,768]{1,0:T(8,128)(2,1)}, u32[]{:S(2)}, u32[]{:S(2)}) collective-permute-start(bf16[870,768]{1,0:T(8,128)(2,1)} %convolution_convert_fusion.3), channel_id=1, source_target_pairs={{0,16},{16,0},{1,17},{17,1},{2,18},{18,2},{3,19},{19,3},{4,20},{20... | collective-permute-start | bytes 4008968 | tf_op jit(solution)/shard_map/ppermute | solution.py:18
  12.3 94.3 %collective-permute-start = (bf16[870,768]{1,0:T(8,128)(2,1)}, bf16[870,768]{1,0:T(8,128)(2,1)}, u32[]{:S(2)}, u32[]{:S(2)}) collective-permute-start(bf16[870,768]{1,0:T(8,128)(2,1)} %convolution_convert_fusion.4), channel_id=1, source_target_pairs={{0,16},{16,0},{1,17},{17,1},{2,18},{18,2},{3,19},{19,3},{4,20},{20... | collective-permute-start | bytes 4008968 | tf_op jit(solution)/shard_map/ppermute | solution.py:18
  389.5 138.6 %collective-permute-start.3 = (bf16[870,768]{1,0:T(8,128)(2,1)}, bf16[870,768]{1,0:T(8,128)(2,1)}, u32[]{:S(2)}, u32[]{:S(2)}) collective-permute-start(bf16[870,768]{1,0:T(8,128)(2,1)} %copy.145), channel_id=1, source_target_pairs={{0,16},{16,0},{1,17},{17,1},{2,18},{18,2},{3,19},{19,3},{4,20},{20... | collective-permute-start | bytes 4008968 | tf_op jit(solution)/shard_map/ppermute | solution.py:18
  393.4 138.5 %collective-permute-start.2 = (bf16[870,768]{1,0:T(8,128)(2,1)}, bf16[870,768]{1,0:T(8,128)(2,1)}, u32[]{:S(2)}, u32[]{:S(2)}) collective-permute-start(bf16[870,768]{1,0:T(8,128)(2,1)} %copy.144), channel_id=1, source_target_pairs={{0,16},{16,0},{1,17},{17,1},{2,18},{18,2},{3,19},{19,3},{4,20},{20... | collective-permute-start | bytes 4008968 | tf_op jit(solution)/shard_map/ppermute | solution.py:18
  397.6 111.1 %collective-permute-start.64 = (bf16[768,768]{1,0:T(8,128)(2,1)}, bf16[768,768]{1,0:T(8,128)(2,1)}, u32[]{:S(2)}, u32[]{:S(2)}) collective-permute-start(bf16[768,768]{1,0:T(8,128)(2,1)} %dynamic-slice_bitcast_fusion.1), channel_id=1, source_target_pairs={{0,1},{1,0},{2,3},{3,2},{4,5},{5,4},{6,7},{7,6},{8,9},{9,8},{10,11... | collective-permute-start | bytes 3538952 | tf_op jit(solution)/shard_map/ppermute | solution.py:121
  399.2 116.6 %collective-permute-start.74 = (bf16[768,768]{1,0:T(8,128)(2,1)}, bf16[768,768]{1,0:T(8,128)(2,1)}, u32[]{:S(2)}, u32[]{:S(2)}) collective-permute-start(bf16[768,768]{1,0:T(8,128)(2,1)} %dynamic-slice_bitcast_fusion), channel_id=1, source_target_pairs={{0,1},{1,0},{2,3},{3,2},{4,5},{5,4},{6,7},{7,6},{8,9},{9,8},{10,11... | collective-permute-start | bytes 3538952 | tf_op jit(solution)/shard_map/ppermute | solution.py:121
  400.8 112.3 %collective-permute-start.44 = (bf16[384,1536]{1,0:T(8,128)(2,1)}, bf16[384,1536]{1,0:T(8,128)(2,1)}, u32[]{:S(2)}, u32[]{:S(2)}) collective-permute-start(bf16[384,1536]{1,0:T(8,128)(2,1)} %dynamic-slice_bitcast_fusion.3), channel_id=1, source_target_pairs={{0,1},{1,0},{2,3},{3,2},{4,5},{5,4},{6,7},{7,6},{8,9},{9,8},{10,11... | collective-permute-start | bytes 3538952 | tf_op jit(solution)/shard_map/ppermute | solution.py:121
  519.0 39.6 %collective-permute-start.65 = (bf16[384,768]{1,0:T(8,128)(2,1)}, bf16[384,768]{1,0:T(8,128)(2,1)}, u32[]{:S(2)}, u32[]{:S(2)}) collective-permute-start(bf16[384,768]{1,0:T(8,128)(2,1)} %dynamic-slice_bitcast_fusion.6), channel_id=1, source_target_pairs={{0,2},{1,3},{2,0},{3,1},{4,6},{5,7},{6,4},{7,5},{8,10},{9,11},{10,... | collective-permute-start | bytes 1769480 | tf_op jit(solution)/shard_map/ppermute | solution.py:121
  521.7 42.5 %collective-permute-start.75 = (bf16[384,768]{1,0:T(8,128)(2,1)}, bf16[384,768]{1,0:T(8,128)(2,1)}, u32[]{:S(2)}, u32[]{:S(2)}) collective-permute-start(bf16[384,768]{1,0:T(8,128)(2,1)} %dynamic-slice_bitcast_fusion.5), channel_id=1, source_target_pairs={{0,16},{16,0},{1,17},{17,1},{2,18},{18,2},{3,19},{19,3},{4,20},{20... | collective-permute-start | bytes 1769480 | tf_op jit(solution)/shard_map/ppermute | solution.py:121
  526.1 29.9 %collective-permute-start.45 = (bf16[192,1536]{1,0:T(8,128)(2,1)}, bf16[192,1536]{1,0:T(8,128)(2,1)}, u32[]{:S(2)}, u32[]{:S(2)}) collective-permute-start(bf16[192,1536]{1,0:T(8,128)(2,1)} %dynamic-slice_bitcast_fusion.8), channel_id=1, source_target_pairs={{0,2},{1,3},{2,0},{3,1},{4,6},{5,7},{6,4},{7,5},{8,10},{9,11},{10,... | collective-permute-start | bytes 1769480 | tf_op jit(solution)/shard_map/ppermute | solution.py:121
  528.1 34.1 %collective-permute-start.55 = (bf16[192,1536]{1,0:T(8,128)(2,1)}, bf16[192,1536]{1,0:T(8,128)(2,1)}, u32[]{:S(2)}, u32[]{:S(2)}) collective-permute-start(bf16[192,1536]{1,0:T(8,128)(2,1)} %dynamic-slice_bitcast_fusion.7), channel_id=1, source_target_pairs={{0,16},{16,0},{1,17},{17,1},{2,18},{18,2},{3,19},{19,3},{4,20},{20... | collective-permute-start | bytes 1769480 | tf_op jit(solution)/shard_map/ppermute | solution.py:121
  532.0 29.1 %collective-permute-start.25 = (bf16[192,1536]{1,0:T(8,128)(2,1)}, bf16[192,1536]{1,0:T(8,128)(2,1)}, u32[]{:S(2)}, u32[]{:S(2)}) collective-permute-start(bf16[192,1536]{1,0:T(8,128)(2,1)} %dynamic-slice_bitcast_fusion.10), channel_id=1, source_target_pairs={{0,2},{1,3},{2,0},{3,1},{4,6},{5,7},{6,4},{7,5},{8,10},{9,11},{10,... | collective-permute-start | bytes 1769480 | tf_op jit(solution)/shard_map/ppermute | solution.py:121
  561.1 38.7 %collective-permute-start.84 = (bf16[512,768]{1,0:T(8,128)(2,1)S(1)}, bf16[512,768]{1,0:T(8,128)(2,1)S(1)}, u32[]{:S(2)}, u32[]{:S(2)}) collective-permute-start(bf16[512,768]{1,0:T(8,128)(2,1)S(1)} %dynamic-slice_bitcast_fusion.4), channel_id=1, source_target_pairs={{0,1},{1,0},{2,3},{3,2},{4,5},{5,4},{6,7},{7,6},{8,9},{9,8},{10,11... | collective-permute-start | bytes 2359304 | tf_op jit(solution)/shard_map/ppermute | solution.py:121
  562.2 120.2 %collective-permute-start.34 = (bf16[384,1536]{1,0:T(8,128)(2,1)}, bf16[384,1536]{1,0:T(8,128)(2,1)}, u32[]{:S(2)}, u32[]{:S(2)}) collective-permute-start(bf16[384,1536]{1,0:T(8,128)(2,1)} %fusion.41), channel_id=1, source_target_pairs={{0,1},{1,0},{2,3},{3,2},{4,5},{5,4},{6,7},{7,6},{8,9},{9,8},{10,11... | collective-permute-start | bytes 3538952 | tf_op jit(solution)/shard_map/ppermute | solution.py:121
  564.1 19.9 %collective-permute-start.66 = (bf16[192,768]{1,0:T(8,128)(2,1)S(1)}, bf16[192,768]{1,0:T(8,128)(2,1)S(1)}, u32[]{:S(2)}, u32[]{:S(2)}) collective-permute-start(bf16[192,768]{1,0:T(8,128)(2,1)S(1)} %dynamic-slice_bitcast_fusion.15), channel_id=1, source_target_pairs={{0,16},{16,0},{1,17},{17,1},{2,18},{18,2},{3,19},{19,3},{4,20},{20... | collective-permute-start | bytes 884744 | tf_op jit(solution)/shard_map/ppermute | solution.py:121
  592.4 21.5 %collective-permute-start.67 = (bf16[96,768]{1,0:T(8,128)(2,1)S(1)}, bf16[96,768]{1,0:T(8,128)(2,1)S(1)}, u32[]{:S(2)}, u32[]{:S(2)}) collective-permute-start(bf16[96,768]{1,0:T(8,128)(2,1)S(1)} %dynamic-slice_bitcast_fusion.24), channel_id=1, source_target_pairs={{0,4},{1,5},{2,6},{3,7},{4,0},{5,1},{6,2},{7,3},{8,12},{9,13},{10,... | collective-permute-start | bytes 442376 | tf_op jit(solution)/shard_map/ppermute | solution.py:121
  613.9 71.7 %collective-permute-start.85 = (bf16[256,768]{1,0:T(8,128)(2,1)}, bf16[256,768]{1,0:T(8,128)(2,1)}, u32[]{:S(2)}, u32[]{:S(2)}) collective-permute-start(bf16[256,768]{1,0:T(8,128)(2,1)} %dynamic-slice_bitcast_fusion.13), channel_id=1, source_target_pairs={{0,2},{1,3},{2,0},{3,1},{4,6},{5,7},{6,4},{7,5},{8,10},{9,11},{10,... | collective-permute-start | bytes 1179656 | tf_op jit(solution)/shard_map/ppermute | solution.py:121
  615.8 19.8 %collective-permute-start.68 = (bf16[48,768]{1,0:T(8,128)(2,1)}, bf16[48,768]{1,0:T(8,128)(2,1)S(1)}, u32[]{:S(2)}, u32[]{:S(2)}) collective-permute-start(bf16[48,768]{1,0:T(8,128)(2,1)} %dynamic-slice_bitcast_fusion.33), channel_id=1, source_target_pairs={{0,8},{1,9},{2,10},{3,11},{4,12},{5,13},{6,14},{7,15},{8,0},{9,1},... | collective-permute-start | bytes 221192 | tf_op jit(solution)/shard_map/ppermute | solution.py:121
  618.4 20.2 %collective-permute-start.78 = (bf16[48,768]{1,0:T(8,128)(2,1)}, bf16[48,768]{1,0:T(8,128)(2,1)S(1)}, u32[]{:S(2)}, u32[]{:S(2)}) collective-permute-start(bf16[48,768]{1,0:T(8,128)(2,1)} %dynamic-slice_bitcast_fusion.32), channel_id=1, source_target_pairs={{0,8},{1,9},{2,10},{3,11},{4,12},{5,13},{6,14},{7,15},{8,0},{9,1},... | collective-permute-start | bytes 221192 | tf_op jit(solution)/shard_map/ppermute | solution.py:121
  676.8 22.2 %collective-permute-start.71 = (bf16[192,768]{1,0:T(8,128)(2,1)S(1)}, bf16[192,768]{1,0:T(8,128)(2,1)S(1)}, u32[]{:S(2)}, u32[]{:S(2)}) collective-permute-start(bf16[192,768]{1,0:T(8,128)(2,1)S(1)} %pad_maximum_fusion.30), channel_id=1, source_target_pairs={{0,16},{16,0},{1,17},{17,1},{2,18},{18,2},{3,19},{19,3},{4,20},{20... | collective-permute-start | bytes 884744 | tf_op jit(solution)/shard_map/ppermute | solution.py:121
  679.7 21.2 %collective-permute-start.81 = (bf16[192,768]{1,0:T(8,128)(2,1)S(1)}, bf16[192,768]{1,0:T(8,128)(2,1)S(1)}, u32[]{:S(2)}, u32[]{:S(2)}) collective-permute-start(bf16[192,768]{1,0:T(8,128)(2,1)S(1)} %pad_maximum_fusion.31), channel_id=1, source_target_pairs={{0,2},{1,3},{2,0},{3,1},{4,6},{5,7},{6,4},{7,5},{8,10},{9,11},{10,... | collective-permute-start | bytes 884744 | tf_op jit(solution)/shard_map/ppermute | solution.py:121
  698.1 28.1 %collective-permute-start.35 = (bf16[192,1536]{1,0:T(8,128)(2,1)S(1)}, bf16[192,1536]{1,0:T(8,128)(2,1)S(1)}, u32[]{:S(2)}, u32[]{:S(2)}) collective-permute-start(bf16[192,1536]{1,0:T(8,128)(2,1)S(1)} %dynamic-slice_bitcast_fusion.9), channel_id=1, source_target_pairs={{0,16},{16,0},{1,17},{17,1},{2,18},{18,2},{3,19},{19,3},{4,20},{20... | collective-permute-start | bytes 1769480 | tf_op jit(solution)/shard_map/ppermute | solution.py:121
  700.8 45.2 %collective-permute-start.72 = (bf16[384,768]{1,0:T(8,128)(2,1)S(1)}, bf16[384,768]{1,0:T(8,128)(2,1)S(1)}, u32[]{:S(2)}, u32[]{:S(2)}) collective-permute-start(bf16[384,768]{1,0:T(8,128)(2,1)S(1)} %pad_maximum_fusion.21), channel_id=1, source_target_pairs={{0,2},{1,3},{2,0},{3,1},{4,6},{5,7},{6,4},{7,5},{8,10},{9,11},{10,... | collective-permute-start | bytes 1769480 | tf_op jit(solution)/shard_map/ppermute | solution.py:121
  705.5 44.7 %collective-permute-start.82 = (bf16[384,768]{1,0:T(8,128)(2,1)S(1)}, bf16[384,768]{1,0:T(8,128)(2,1)S(1)}, u32[]{:S(2)}, u32[]{:S(2)}) collective-permute-start(bf16[384,768]{1,0:T(8,128)(2,1)S(1)} %pad_maximum_fusion.22), channel_id=1, source_target_pairs={{0,16},{16,0},{1,17},{17,1},{2,18},{18,2},{3,19},{19,3},{4,20},{20... | collective-permute-start | bytes 1769480 | tf_op jit(solution)/shard_map/ppermute | solution.py:121
  706.5 39.4 %collective-permute-start.52 = (bf16[192,1536]{1,0:T(8,128)(2,1)S(1)}, bf16[192,1536]{1,0:T(8,128)(2,1)S(1)}, u32[]{:S(2)}, u32[]{:S(2)}) collective-permute-start(bf16[192,1536]{1,0:T(8,128)(2,1)S(1)} %pad_maximum_fusion.19), channel_id=1, source_target_pairs={{0,2},{1,3},{2,0},{3,1},{4,6},{5,7},{6,4},{7,5},{8,10},{9,11},{10,... | collective-permute-start | bytes 1769480 | tf_op jit(solution)/shard_map/ppermute | solution.py:121
  724.2 26.9 %collective-permute-start.62 = (bf16[192,1536]{1,0:T(8,128)(2,1)S(1)}, bf16[192,1536]{1,0:T(8,128)(2,1)S(1)}, u32[]{:S(2)}, u32[]{:S(2)}) collective-permute-start(bf16[192,1536]{1,0:T(8,128)(2,1)S(1)} %pad_maximum_fusion.20), channel_id=1, source_target_pairs={{0,16},{16,0},{1,17},{17,1},{2,18},{18,2},{3,19},{19,3},{4,20},{20... | collective-permute-start | bytes 1769480 | tf_op jit(solution)/shard_map/ppermute | solution.py:121
  751.0 74.3 %collective-permute-start.73 = (bf16[768,768]{1,0:T(8,128)(2,1)}, bf16[768,768]{1,0:T(8,128)(2,1)}, u32[]{:S(2)}, u32[]{:S(2)}) collective-permute-start(bf16[768,768]{1,0:T(8,128)(2,1)} %pad_maximum_fusion.12), channel_id=1, source_target_pairs={{0,1},{1,0},{2,3},{3,2},{4,5},{5,4},{6,7},{7,6},{8,9},{9,8},{10,11... | collective-permute-start | bytes 3538952 | tf_op jit(solution)/shard_map/ppermute | solution.py:121
  752.8 75.0 %collective-permute-start.83 = (bf16[768,768]{1,0:T(8,128)(2,1)}, bf16[768,768]{1,0:T(8,128)(2,1)}, u32[]{:S(2)}, u32[]{:S(2)}) collective-permute-start(bf16[768,768]{1,0:T(8,128)(2,1)} %pad_maximum_fusion.13), channel_id=1, source_target_pairs={{0,1},{1,0},{2,3},{3,2},{4,5},{5,4},{6,7},{7,6},{8,9},{9,8},{10,11... | collective-permute-start | bytes 3538952 | tf_op jit(solution)/shard_map/ppermute | solution.py:121
  755.7 74.3 %collective-permute-start.53 = (bf16[384,1536]{1,0:T(8,128)(2,1)}, bf16[384,1536]{1,0:T(8,128)(2,1)}, u32[]{:S(2)}, u32[]{:S(2)}) collective-permute-start(bf16[384,1536]{1,0:T(8,128)(2,1)} %pad_maximum_fusion.10), channel_id=1, source_target_pairs={{0,1},{1,0},{2,3},{3,2},{4,5},{5,4},{6,7},{7,6},{8,9},{9,8},{10,11... | collective-permute-start | bytes 3538952 | tf_op jit(solution)/shard_map/ppermute | solution.py:121
  764.7 70.4 %collective-permute-start.63 = (bf16[384,1536]{1,0:T(8,128)(2,1)}, bf16[384,1536]{1,0:T(8,128)(2,1)}, u32[]{:S(2)}, u32[]{:S(2)}) collective-permute-start(bf16[384,1536]{1,0:T(8,128)(2,1)} %pad_maximum_fusion.11), channel_id=1, source_target_pairs={{0,1},{1,0},{2,3},{3,2},{4,5},{5,4},{6,7},{7,6},{8,9},{9,8},{10,11... | collective-permute-start | bytes 3538952 | tf_op jit(solution)/shard_map/ppermute | solution.py:121
  827.8 30.0 %collective-permute-start.42 = (bf16[192,1536]{1,0:T(8,128)(2,1)}, bf16[192,1536]{1,0:T(8,128)(2,1)}, u32[]{:S(2)}, u32[]{:S(2)}) collective-permute-start(bf16[192,1536]{1,0:T(8,128)(2,1)} %pad_maximum_fusion.18), channel_id=1, source_target_pairs={{0,16},{16,0},{1,17},{17,1},{2,18},{18,2},{3,19},{19,3},{4,20},{20... | collective-permute-start | bytes 1769480 | tf_op jit(solution)/shard_map/ppermute | solution.py:121
  830.0 29.3 %collective-permute-start.32 = (bf16[192,1536]{1,0:T(8,128)(2,1)}, bf16[192,1536]{1,0:T(8,128)(2,1)}, u32[]{:S(2)}, u32[]{:S(2)}) collective-permute-start(bf16[192,1536]{1,0:T(8,128)(2,1)} %pad_maximum_fusion.17), channel_id=1, source_target_pairs={{0,2},{1,3},{2,0},{3,1},{4,6},{5,7},{6,4},{7,5},{8,10},{9,11},{10,... | collective-permute-start | bytes 1769480 | tf_op jit(solution)/shard_map/ppermute | solution.py:121
  (215 other events, 1543.3 us)

commit v2 on v1

--- a/solution.py
+++ b/solution.py
@@ -1,11 +1,21 @@
+import functools
+
 import jax
 import jax.numpy as jnp
 from jax import lax
+from jax.experimental import pallas as pl
+from jax.experimental.pallas import tpu as pltpu
 from jax.sharding import PartitionSpec as P
 
-HEADS = 12
 HEAD_DIM = 64
 TOK_DEV = 768
+PATCH_ROWS = 160
+LONGEST = 40
+WINDOW = 64
+SLOTS = 128
+LANES = 256
+BASES = (0, 128, 384, 512)
+TOGETHER = 4
 
 
 def from_partner(block, axis, bit):
@@ -44,76 +54,285 @@
     )
 
 
-def split_heads(values):
-    return values.reshape(values.shape[0], HEADS, HEAD_DIM)
-
-
-def head_scores(queries, keys_in, allowed):
-    raw_scores = jnp.einsum(
-        "qhd,khd->hqk",
-        split_heads(queries),
-        split_heads(keys_in),
-        preferred_element_type=jnp.float32,
-    ) * HEAD_DIM ** (-0.5)
-    return jnp.where(allowed[None], raw_scores, -1e30)
-
-
-def attend_forward(queries, keys_in, values_in, allowed):
-    scores = head_scores(queries, keys_in, allowed)
-    row_top = jnp.max(scores, axis=-1, keepdims=True)
-    exp_scores = jnp.exp(scores - row_top)
-    row_total = jnp.sum(exp_scores, axis=-1, keepdims=True)
-    softmax_out = (exp_scores / row_total).astype(jnp.bfloat16)
-    mixed_heads = jnp.einsum(
-        "hqk,khd->qhd", softmax_out, split_heads(values_in), preferred_element_type=jnp.float32
-    )
-    return (mixed_heads.reshape(queries.shape[0], -1), row_top + jnp.log(row_total))
-
-
-def attend_backward(queries, keys_in, values_in, allowed, log_total, grad_mixed):
-    scores = head_scores(queries, keys_in, allowed)
-    softmax_out = jnp.exp(scores - log_total)
-    grad_heads = split_heads(grad_mixed)
-    grad_soft = jnp.einsum(
-        "qhd,khd->hqk", grad_heads, split_heads(values_in), preferred_element_type=jnp.float32
-    )
-    row_inner = jnp.sum(softmax_out * grad_soft, axis=-1, keepdims=True)
-    grad_scores = (softmax_out * (grad_soft - row_inner)).astype(jnp.bfloat16)
-    grad_queries = jnp.einsum(
-        "hqk,khd->qhd", grad_scores, split_heads(keys_in), preferred_element_type=jnp.float32
-    ) * HEAD_DIM ** (-0.5)
-    grad_keys = jnp.einsum(
-        "hqk,qhd->khd", grad_scores, split_heads(queries), preferred_element_type=jnp.float32
-    ) * HEAD_DIM ** (-0.5)
-    grad_values = jnp.einsum(
-        "hqk,qhd->khd",
-        softmax_out.astype(jnp.bfloat16),
-        grad_heads,
-        preferred_element_type=jnp.float32,
-    )
-    return (
-        grad_queries.reshape(queries.shape[0], -1).astype(jnp.bfloat16),
-        grad_keys.reshape(keys_in.shape[0], -1).astype(jnp.bfloat16),
-        grad_values.reshape(keys_in.shape[0], -1).astype(jnp.bfloat16),
-    )
-
-
-def block_masks(row_lengths, row_images, row_boxes, image_count):
-    row_ends = jnp.cumsum(row_lengths)
-    position = jnp.arange(TOK_DEV, dtype=jnp.int32)
-    row_of = jnp.sum((position[:, None] >= row_ends[None, :]).astype(jnp.int32), axis=1)
-    same_row = row_of[:, None] == row_of[None, :]
-    choose = (row_of[:, None] == jnp.arange(row_lengths.shape[0], dtype=jnp.int32)[None, :]).astype(
-        jnp.int32
-    )
-    token_image = jnp.sum(choose * row_images[None, :], axis=1)
-    token_box = jnp.sum(choose[:, :, None] * row_boxes[None, :, :], axis=1)
-    patch_count = row_boxes.shape[1]
-    key_image = jnp.arange(image_count * patch_count, dtype=jnp.int32) // patch_count
-    cross_allowed = (token_image[:, None] == key_image[None, :]) & (
-        jnp.tile(token_box, (1, image_count)) > 0
-    )
-    return (same_row, cross_allowed)
+def slot_of(shape, dim):
+    slot = lax.broadcasted_iota(jnp.int32, shape, dim)
+    part = (slot >= LONGEST).astype(jnp.int32) + (slot >= 2 * LONGEST).astype(jnp.int32)
+    return part, slot - part * LONGEST
+
+
+def fill_head_masks(masks_ref):
+    part, _ = slot_of((SLOTS, LANES), 0)
+    lane = lax.broadcasted_iota(jnp.int32, (SLOTS, LANES), 1)
+    for odd in range(2):
+        low = HEAD_DIM * (part + odd)
+        inside = (lane >= low) & (lane < low + HEAD_DIM)
+        masks_ref[odd] = jnp.where(inside, 1.0, 0.0).astype(jnp.bfloat16)
+
+
+def row_place(start):
+    first = jnp.minimum(lax.bitwise_and(start, -16), TOK_DEV - WINDOW)
+    return pl.multiple_of(first, 16), start - first
+
+
+def pick_rows(offset, length):
+    _, place = slot_of((SLOTS, WINDOW), 0)
+    at = lax.broadcasted_iota(jnp.int32, (SLOTS, WINDOW), 1)
+    return jnp.where((place < length) & (at == place + offset), 1.0, 0.0).astype(jnp.bfloat16)
+
+
+def put_rows(offset, length):
+    _, place = slot_of((WINDOW, SLOTS), 1)
+    at = lax.broadcasted_iota(jnp.int32, (WINDOW, SLOTS), 0)
+    return jnp.where((place < length) & (at == place + offset), 1.0, 0.0).astype(jnp.bfloat16)
+
+
+def dot(left, right, over):
+    return lax.dot_general(left, right, (over, ((), ())), preferred_element_type=jnp.float32)
+
+
+NT = ((1,), (1,))
+NN = ((1,), (0,))
+TN = ((0,), (0,))
+
+
+def side_by_side(parts):
+    first, second, third, fourth = parts
+    half = LANES // 2
+    return jnp.concatenate(
+        [
+            first[:, :half],
+            first[:, half:] + second[:, :half],
+            second[:, half:],
+            third[:, :half],
+            third[:, half:] + fourth[:, :half],
+            fourth[:, half:],
+        ],
+        axis=1,
+    )
+
+
+def self_allowed(offset, length):
+    at = lax.broadcasted_iota(jnp.int32, (WINDOW, SLOTS), 0)
+    return (at >= offset) & (at < offset + length)
+
+
+def cross_allowed(box_ref, row):
+    turn = lax.broadcasted_iota(jnp.int32, (SLOTS, SLOTS), 0)
+    chosen = jnp.where(turn == row, 1.0, 0.0).astype(jnp.bfloat16)
+    return dot(box_ref[...], chosen, NN) > 0.5
+
+
+def row_keys(cross, first, image, ref, base):
+    if cross:
+        return ref[image, :, base : base + LANES]
+    return ref[pl.ds(first, WINDOW), base : base + LANES]
+
+
+def forward_kernel(cross, *refs):
+    if cross:
+        lengths, images, box_ref, q_ref, k_ref, v_ref, out_ref, log_ref, masks, total = refs
+    else:
+        lengths, q_ref, k_ref, v_ref, out_ref, log_ref, masks, total = refs
+        images = box_ref = None
+    fill_head_masks(masks)
+    total[...] = jnp.zeros_like(total)
+
+    def rows_at_once(step, start):
+        work = []
+        for turn in range(TOGETHER):
+            row = TOGETHER * step + turn
+            length = lengths[0, row]
+            first, offset = row_place(start)
+            work.append((row, length, images[0, row] if cross else None, first, offset))
+            start = start + length
+        picked = [
+            dot(pick_rows(offset, length), q_ref[pl.ds(first, WINDOW), :], NN)
+            for _, length, _, first, offset in work
+        ]
+        picked = [(p * HEAD_DIM ** (-0.5)).astype(jnp.bfloat16) for p in picked]
+        allowed = [
+            cross_allowed(box_ref, row) if cross else self_allowed(offset, length)
+            for row, length, _, _, offset in work
+        ]
+        each = [(turn, group) for turn in range(TOGETHER) for group in range(len(BASES))]
+        scores = {}
+        for turn, group in each:
+            _, _, image, first, _ = work[turn]
+            base = BASES[group]
+            queries = picked[turn][:, base : base + LANES] * masks[group % 2]
+            keys_in = row_keys(cross, first, image, k_ref, base)
+            scores[turn, group] = dot(keys_in, queries, NT)
+        soft = {}
+        for turn, group in each:
+            row = work[turn][0]
+            masked = jnp.where(allowed[turn], scores[turn, group], -1e30)
+            top = jnp.max(masked, axis=0, keepdims=True)
+            exps = jnp.exp(masked - top)
+            summed = jnp.sum(exps, axis=0, keepdims=True)
+            soft[turn, group] = (exps * (1.0 / summed)).astype(jnp.bfloat16)
+            log_ref[row, group : group + 1, :] = top + jnp.log(summed)
+        mixed = {}
+        for turn, group in each:
+            _, _, image, first, _ = work[turn]
+            values_in = row_keys(cross, first, image, v_ref, BASES[group])
+            mixed[turn, group] = (
+                dot(soft[turn, group], values_in, TN).astype(jnp.bfloat16) * masks[group % 2]
+            )
+        for turn in range(TOGETHER):
+            _, length, _, first, offset = work[turn]
+            side = side_by_side([mixed[turn, group] for group in range(len(BASES))])
+            total[pl.ds(first, WINDOW), :] += dot(put_rows(offset, length), side, NN)
+        return start
+
+    rows = lengths.shape[1]
+    lax.fori_loop(0, rows // TOGETHER, rows_at_once, jnp.int32(0))
+    out_ref[...] = total[...].astype(out_ref.dtype)
+
+
+def backward_kernel(cross, *refs):
+    if cross:
+        lengths, images, box_ref = refs[:3]
+        refs = refs[3:]
+    else:
+        lengths, refs = refs[0], refs[1:]
+        images = box_ref = None
+    q_ref, k_ref, v_ref, g_ref, log_ref, dq_ref, dk_ref, dv_ref, masks, dq, dk, dv = refs
+    fill_head_masks(masks)
+    dq[...] = jnp.zeros_like(dq)
+    dk[...] = jnp.zeros_like(dk)
+    dv[...] = jnp.zeros_like(dv)
+
+    def rows_at_once(step, start):
+        work = []
+        for turn in range(TOGETHER):
+            row = TOGETHER * step + turn
+            length = lengths[0, row]
+            first, offset = row_place(start)
+            work.append((row, length, images[0, row] if cross else None, first, offset))
+            start = start + length
+        picks = [pick_rows(offset, length) for _, length, _, _, offset in work]
+        picked = [
+            (dot(pick, q_ref[pl.ds(w[3], WINDOW), :], NN) * HEAD_DIM ** (-0.5)).astype(jnp.bfloat16)
+            for pick, w in zip(picks, work)
+        ]
+        picked_g = [
+            dot(pick, g_ref[pl.ds(w[3], WINDOW), :], NN).astype(jnp.bfloat16)
+            for pick, w in zip(picks, work)
+        ]
+        allowed = [
+            cross_allowed(box_ref, row) if cross else self_allowed(offset, length)
+            for row, length, _, _, offset in work
+        ]
+        each = [(turn, group) for turn in range(TOGETHER) for group in range(len(BASES))]
+        queries, grads, scores, grad_soft = {}, {}, {}, {}
+        for turn, group in each:
+            _, _, image, first, _ = work[turn]
+            base = BASES[group]
+            mask = masks[group % 2]
+            queries[turn, group] = picked[turn][:, base : base + LANES] * mask
+            grads[turn, group] = picked_g[turn][:, base : base + LANES] * mask
+            keys_in = row_keys(cross, first, image, k_ref, base)
+            values_in = row_keys(cross, first, image, v_ref, base)
+            scores[turn, group] = dot(keys_in, queries[turn, group], NT)
+            grad_soft[turn, group] = dot(values_in, grads[turn, group], NT)
+        soft, grad_scores = {}, {}
+        for turn, group in each:
+            row = work[turn][0]
+            masked = jnp.where(allowed[turn], scores[turn, group], -1e30)
+            kept = jnp.exp(masked - log_ref[row, group : group + 1, :])
+            inner = jnp.sum(kept * grad_soft[turn, group], axis=0, keepdims=True)
+            grad_scores[turn, group] = (kept * (grad_soft[turn, group] - inner)).astype(
+                jnp.bfloat16
+            )
+            soft[turn, group] = kept.astype(jnp.bfloat16)
+        grad_k, grad_v, grad_q = {}, {}, {}
+        for turn, group in each:
+            _, _, image, first, _ = work[turn]
+            keys_in = row_keys(cross, first, image, k_ref, BASES[group])
+            grad_k[turn, group] = dot(grad_scores[turn, group], queries[turn, group], NN)
+            grad_v[turn, group] = dot(soft[turn, group], grads[turn, group], NN)
+            grad_q[turn, group] = (
+                dot(grad_scores[turn, group], keys_in, TN) * HEAD_DIM ** (-0.5)
+            ).astype(jnp.bfloat16) * masks[group % 2]
+        for turn in range(TOGETHER):
+            _, length, image, first, offset = work[turn]
+            every = range(len(BASES))
+            side_k = side_by_side([grad_k[turn, group] for group in every])
+            side_v = side_by_side([grad_v[turn, group] for group in every])
+            side_q = side_by_side([grad_q[turn, group] for group in every])
+            if cross:
+                dk[image] += side_k
+                dv[image] += side_v
+            else:
+                dk[pl.ds(first, WINDOW), :] += side_k
+                dv[pl.ds(first, WINDOW), :] += side_v
+            dq[pl.ds(first, WINDOW), :] += dot(put_rows(offset, length), side_q, NN)
+        return start
+
+    rows = lengths.shape[1]
+    lax.fori_loop(0, rows // TOGETHER, rows_at_once, jnp.int32(0))
+    dq_ref[...] = dq[...].astype(dq_ref.dtype)
+    dk_ref[...] = dk[...].astype(dk_ref.dtype)
+    dv_ref[...] = dv[...].astype(dv_ref.dtype)
+
+
+def in_smem():
+    return pl.BlockSpec(memory_space=pltpu.SMEM)
+
+
+def in_vmem():
+    return pl.BlockSpec(memory_space=pltpu.VMEM)
+
+
+def attend(scalars, queries, keys_in, values_in, box):
+    cross = box is not None
+    rows = scalars[0].shape[1]
+    tensors = ((box,) if cross else ()) + (queries, keys_in, values_in)
+    return pl.pallas_call(
+        functools.partial(forward_kernel, cross),
+        out_shape=(
+            jax.ShapeDtypeStruct(queries.shape, jnp.bfloat16),
+            jax.ShapeDtypeStruct((rows, len(BASES), SLOTS), jnp.float32),
+        ),
+        in_specs=[in_smem()] * len(scalars) + [in_vmem()] * len(tensors),
+        out_specs=(in_vmem(), in_vmem()),
+        scratch_shapes=[
+            pltpu.VMEM((2, SLOTS, LANES), jnp.bfloat16),
+            pltpu.VMEM(queries.shape, jnp.float32),
+        ],
+        compiler_params=pltpu.CompilerParams(vmem_limit_bytes=40 << 20),
+        cost_estimate=pl.CostEstimate(flops=8 << 30, bytes_accessed=6 << 20, transcendentals=1 << 21),
+        name="cross_attend" if cross else "self_attend",
+    )(*scalars, *tensors)
+
+
+def attend_back(scalars, queries, keys_in, values_in, grads, logs, box):
+    cross = box is not None
+    tensors = ((box,) if cross else ()) + (queries, keys_in, values_in, grads, logs)
+    return pl.pallas_call(
+        functools.partial(backward_kernel, cross),
+        out_shape=tuple(
+            jax.ShapeDtypeStruct(a.shape, jnp.bfloat16) for a in (queries, keys_in, values_in)
+        ),
+        in_specs=[in_smem()] * len(scalars) + [in_vmem()] * len(tensors),
+        out_specs=(in_vmem(),) * 3,
+        scratch_shapes=[
+            pltpu.VMEM((2, SLOTS, LANES), jnp.bfloat16),
+            pltpu.VMEM(queries.shape, jnp.float32),
+            pltpu.VMEM(keys_in.shape, jnp.float32),
+            pltpu.VMEM(keys_in.shape, jnp.float32),
+        ],
+        compiler_params=pltpu.CompilerParams(vmem_limit_bytes=48 << 20),
+        cost_estimate=pl.CostEstimate(flops=20 << 30, bytes_accessed=12 << 20, transcendentals=1 << 21),
+        name="cross_attend_back" if cross else "self_attend_back",
+    )(*scalars, *tensors)
+
+
+def box_columns(box_mask, patch_rows):
+    turned = jnp.transpose(box_mask).astype(jnp.bfloat16)
+    return jnp.pad(
+        turned, ((0, patch_rows - turned.shape[0]), (0, SLOTS - turned.shape[1]))
+    )
 
 
 def flip_bit(values, axis, bit):
@@ -170,6 +389,13 @@
         values = jnp.concatenate(
             [jnp.where(low, values, other), jnp.where(low, other, values)], axis=dims[step]
         )
+    return values
+
+
+def sum_everywhere(values):
+    order, _ = stage_orders()
+    for axis, bit in order:
+        values = values + flip_bit(values, axis, bit)
     return values
 
 
@@ -204,8 +430,15 @@
     vision_proj,
 ):
     image_count = patches.shape[0]
-    same_row, cross_allowed = block_masks(lengths[0], row_image[0], box_mask[0], image_count)
-    flat_patches = patches.reshape(image_count * patches.shape[1], patches.shape[2])
+    box = box_columns(box_mask[0], PATCH_ROWS)
+    patch_count = patches.shape[1]
+    flat_patches = jnp.pad(patches, ((0, 0), (0, PATCH_ROWS - patch_count), (0, 0))).reshape(
+        image_count * PATCH_ROWS, patches.shape[2]
+    )
+
+    def by_image(values):
+        return values.reshape(image_count, PATCH_ROWS, values.shape[-1])
+
     projected = matmul(flat_patches, vision_proj).astype(jnp.bfloat16)
     own_keys = matmul(projected, cross_key).astype(jnp.bfloat16)
     own_values = matmul(projected, cross_value).astype(jnp.bfloat16)
@@ -213,14 +446,13 @@
     query_s = matmul(text_tokens, self_query).astype(jnp.bfloat16)
     key_s = matmul(text_tokens, self_key).astype(jnp.bfloat16)
     value_s = matmul(text_tokens, self_value).astype(jnp.bfloat16)
-    attended, self_log = attend_forward(query_s, key_s, value_s, same_row)
-    attended_b = attended.astype(jnp.bfloat16)
+    attended_b, self_log = attend((lengths,), query_s, key_s, value_s, None)
     first_sum = text_tokens.astype(jnp.float32) + matmul(attended_b, self_output)
     normed_one, first_back = jax.vjp(norm_rows, first_sum, first_gain, first_bias)
     normed_one_b = normed_one.astype(jnp.bfloat16)
     query_c = matmul(normed_one_b, cross_query).astype(jnp.bfloat16)
-    crossed, cross_log = attend_forward(query_c, far_keys, far_values, cross_allowed)
-    crossed_b = crossed.astype(jnp.bfloat16)
+    far_keys, far_values = by_image(far_keys), by_image(far_values)
+    crossed_b, cross_log = attend((lengths, row_image), query_c, far_keys, far_values, box)
     second_sum = normed_one + matmul(crossed_b, cross_output)
     normed_two, second_back = jax.vjp(norm_rows, second_sum, second_gain, second_bias)
     normed_two_b = normed_two.astype(jnp.bfloat16)
@@ -241,17 +473,19 @@
     grad_second_b = grad_second.astype(jnp.bfloat16)
     grad_cross_output = matmul_left_t(crossed_b, grad_second_b)
     grad_crossed = matmul_right_t(grad_second_b, cross_output).astype(jnp.bfloat16)
-    grad_query_c, grad_far_keys, grad_far_values = attend_backward(
-        query_c, far_keys, far_values, cross_allowed, cross_log, grad_crossed
-    )
+    grad_query_c, grad_far_keys, grad_far_values = attend_back(
+        (lengths, row_image), query_c, far_keys, far_values, grad_crossed, cross_log, box
+    )
+    grad_far_keys = grad_far_keys.reshape(projected.shape)
+    grad_far_values = grad_far_values.reshape(projected.shape)
     grad_cross_query = matmul_left_t(normed_one_b, grad_query_c)
     grad_normed_one = grad_second + matmul_right_t(grad_query_c, cross_query)
     grad_first, grad_first_gain, grad_first_bias = first_back(grad_normed_one)
     grad_first_b = grad_first.astype(jnp.bfloat16)
     grad_self_output = matmul_left_t(attended_b, grad_first_b)
     grad_attended = matmul_right_t(grad_first_b, self_output).astype(jnp.bfloat16)
-    grad_query_s, grad_key_s, grad_value_s = attend_backward(
-        query_s, key_s, value_s, same_row, self_log, grad_attended
+    grad_query_s, grad_key_s, grad_value_s = attend_back(
+        (lengths,), query_s, key_s, value_s, grad_attended, self_log, None
     )
     grad_self_query = matmul_left_t(text_tokens, grad_query_s)
     grad_self_key = matmul_left_t(text_tokens, grad_key_s)
@@ -269,7 +503,7 @@
         matmul_right_t(back_keys, cross_key) + matmul_right_t(back_values, cross_value)
     ).astype(jnp.bfloat16)
     grad_vision = matmul_left_t(flat_patches, grad_projected)
-    patch_grad = matmul_right_t(grad_projected, vision_proj).reshape(patches.shape)
+    patch_grad = by_image(matmul_right_t(grad_projected, vision_proj))[:, :patch_count]
     one_way, other_way = stage_orders()
     half_ff = grad_reduce.shape[0] // 2
     sum_reduce = jnp.concatenate(
@@ -290,7 +524,7 @@
     sum_vision = total(grad_vision, one_way)
     sum_self_output, sum_self_query = couple(grad_self_output, grad_self_query, other_way)
     sum_self_key, sum_self_value = couple(grad_self_key, grad_self_value, one_way)
-    small = lax.psum(
+    small = sum_everywhere(
         jnp.stack(
             [
                 grad_first_gain,
@@ -300,8 +534,7 @@
                 grad_third_gain,
                 grad_third_bias,
             ]
-        ),
-        ("mod", "dp"),
+        )
     )
     return (
         merged,

time: 881 us -> 682 us (0.77)
  matrix products: 307 us -> 125 us
  waiting for transfers between devices: 154 us -> 267 us
  other arithmetic: 171 us -> 86.1 us
  blocking collectives: 77.6 us -> 0 us
  Pallas kernels: 0 us -> 50.8 us
  local copies, waits for them, and re-layouts: 68.9 us -> 50.9 us
    dot_general x12 -> x0, matrix products: 171 us -> none  [the longest x2 48.8 us: attend_backward(): jnp.einsum('qhd,khd->hqk', grad_heads, split_heads(values_in), preferred_...]
    ppermute x4, waiting for transfers between devices: 0.01 us -> 92.1 us  [from_partner(): return lax.ppermute(block, axis, route)]
    psum x1 -> x0, blocking collectives: 77.6 us -> none  [on_device(): lax.psum(jnp.stack([grad_first_gain, grad_first_bias, grad_second_gain, g...]
    convert_element_type x4 -> x1, other arithmetic: 51.9 us -> 0.01 us  [box_columns(): turned = jnp.transpose(box_mask).astype(jnp.bfloat16)]
    pallas_call x0 -> x4, Pallas kernels: none -> 50.8 us  [the longest x2 33.6 us: attend_back(): pl.pallas_call(functools.partial(backward_kernel, cross), out_shape=tuple...]
    reduce_sum x5 -> x0, other arithmetic: 28.8 us -> none  [the longest x2 25.5 us: attend_forward(): row_total = jnp.sum(exp_scores, axis=-1, keepdims=True)]
    ppermute x90 -> x95, waiting for transfers between devices: 154 us -> 174 us  [flip_bit(): return lax.ppermute(values, axis, [(i, i ^ 1 << bit) for i in range(count)])]
    dot_general x11, matrix products: 40 us -> 28.5 us  [matmul_left_t(): lax.dot_general(left, right, (((0,), (0,)), ((), ())), preferred_element_...]
  transfers between devices with their start and end apart: 94 -> 99, of which waited for: 40 -> 53; matrix products, arithmetic and copies ran while one was open for 28% -> 21% of each run, Pallas kernels for 0% -> 1%
where the time goes in v2:
time: 682 us; the launch traced here: 676 us
  waiting for transfers between devices  267 us (39%)
  matrix products  125 us (18%)
  starting transfers between devices  92.7 us (14%)
  other arithmetic  86.1 us (13%)
  local copies, waits for them, and re-layouts  50.9 us (7%)
  Pallas kernels  50.8 us (7%)
    ppermute x95, waiting for transfers between devices, flip_bit(): return lax.ppermute(values, axis, [(i, i ^ 1 << bit) for i in range(count)])  174 us
    ppermute x4, waiting for transfers between devices, from_partner(): return lax.ppermute(block, axis, route)  92.1 us
    ppermute x95, starting transfers between devices, flip_bit(): return lax.ppermute(values, axis, [(i, i ^ 1 << bit) for i in range(count)])  87.1 us
    dot_general x11, matrix products, matmul(): return jnp.dot(left, right, preferred_element_type=jnp.float32)  54 us
    dot_general x11, matrix products, matmul_right_t(): lax.dot_general(left, right, (((1,), (1,)), ((), ())), preferred_element_...  42.7 us
    pallas_call x2, Pallas kernels, attend_back(): pl.pallas_call(functools.partial(backward_kernel, cross), out_shape=tuple...  33.6 us
    dot_general x11, matrix products, matmul_left_t(): lax.dot_general(left, right, (((0,), (0,)), ((), ())), preferred_element_...  28.5 us
    unnamed x255, local copies, waits for them, and re-layouts  23.9 us
  transfers between devices with their start and end apart: 99, of which 53 were waited for; matrix products, arithmetic and copies ran while one was open for 21% of the time, Pallas kernels for 1%

profile of v2, /device:TPU:0, one launch (start us, length us, event | category | flops | bytes accessed | tf_op | source)
XLA Modules:
  0.0 675.7 jit_solution(4795073226262880492)
XLA Ops:
  18.2 7.7 %self_attend.1 = (bf16[768,768]{1,0:T(8,128)(2,1)S(1)}, f32[24,4,128]{2,1,0:T(4,128)S(1)}) custom-call(s32[1,24]{1,0:T(1,128)S(1)} %copy-done.5, bf16[768,768]{1,0:T(8,128)(2,1)S(1)} %convolution_convert_fusion.19.refs_1_, bf16[768,768]{1,0:T(8,128)(2,1)S(1)} %convolution_convert_fusion.18.refs_2_, bf16[768,768]{1,0:T(8,128)(2,1)S(1)} %convolution_convert_fusion.17.refs_3_), custom_call_target="tpu_custom_call" | custom-call | flops 8589934592 | bytes 6291456 | tf_op jit(solution)/shard_map/self_attend/pallas_call | solution.py:291
  37.5 5.7 collective-permute-done
  43.2 30.9 %collective-permute-done.1 = bf16[960,768]{1,0:T(8,128)(2,1)} collective-permute-done((bf16[960,768]{1,0:T(8,128)(2,1)}, bf16[960,768]{1,0:T(8,128)(2,1)}, u32[]{:S(2)}, u32[]{:S(2)}) %collective-permute-start.1) | collective-permute-done | bytes 1474592 | tf_op jit(solution)/shard_map/ppermute | solution.py:28
  74.1 9.6 %cross_attend.1 = (bf16[768,768]{1,0:T(8,128)(2,1)S(1)}, f32[24,4,128]{2,1,0:T(4,128)S(1)}) custom-call(s32[1,24]{1,0:T(1,128)S(1)} %copy-done.5, s32[1,24]{1,0:T(1,128)S(1)} %copy-done.4, bf16[160,128]{1,0:T(8,128)(2,1)S(1)} %pad.8.refs_2_, bf16[768,768]{1,0:T(8,128)(2,1)S(1)} %convolution_convert_fusion.16.refs_3_, bf16[6,160,768]{2,1,0:T(8,128)(2,1)S(1)} %bitcast.310, ...), custom_call_target="tpu_custom_call" | custom-call | flops 8589934592 | bytes 6291456 | tf_op jit(solution)/shard_map/cross_attend/pallas_call | solution.py:291
  85.9 29.5 %multiply_convert_fusion = (bf16[768,3072]{1,0:T(8,128)(2,1)}, f32[768,3072]{1,0:T(8,128)}, f32[768,3072]{1,0:T(8,128)}) fusion(bf16[768,3072]{1,0:T(8,128)(2,1)} %param.41, f32[768,768]{0,1:T(8,128)S(1)} %get-tuple-element.243, f32[768]{0:T(1024)S(1)} %copy-done.110, f32[768]{0:T(1024)S(1)} %copy-done.95, f32[768]{0:T(1024)S(1)} %fusion.40, ...), kind=kOutput, calls=%fused_computation.5 | convolution fusion | flops 3780182016 | bytes 30683136 | tf_op jit(solution)/shard_map/dot_general | solution.py:42
  115.5 7.0 %fusion.55 = (f32[768]{0:T(1024)S(1)}, f32[768,768]{0,1:T(8,128)S(1)}) fusion(bf16[768,3072]{1,0:T(8,128)(2,1)} %get-tuple-element.121, bf16[3072,768]{1,0:T(8,128)(2,1)S(1)} %bitcast.411, f32[768]{0:T(1024)S(1)} %copy-done.110, f32[768]{0:T(1024)S(1)} %copy-done.95, f32[768]{0:T(1024)S(1)} %fusion.40, f32[768,768]{0,1:T(8,128)S(1)} %get-tuple-element.243, ...), kind=kOutput, calls=%fused_computation.375 | convolution fusion | flops 3627416832 | bytes 14171136 | tf_op jit(solution)/shard_map/dot_general | solution.py:42
  126.1 6.6 convolution_convert_fusion
  132.8 15.3 %add_convert_fusion = bf16[768,3072]{1,0:T(8,128)(2,1)} fusion(f32[768,3072]{1,0:T(8,128)} %get-tuple-element.122, f32[768,3072]{1,0:T(8,128)} %get-tuple-element.244, bf16[3072,768]{1,0:T(8,128)(2,1)} %param.42, f32[768]{0:T(1024)S(1)} %negate_multiply_fusion.3, bf16[768,768]{0,1:T(8,128)(2,1)S(1)} %copy-done.15, f32[768,768]{0,1:T(8,128)} %copy-done.24, ...), kind=kOutput, calls=%fused_computation.4 | convolution fusion | flops 3662217216 | bytes 31865856 | tf_op jit(solution)/shard_map/dot_general | solution.py:52
  148.0 10.1 %multiply_reduce_fusion = (f32[768]{0:T(1024)S(1)}, f32[768]{0:T(1024)S(1)}, f32[768]{0:T(1024)S(1)}, f32[768,768]{0,1:T(8,128)S(1)}) fusion(f32[768,768]{0,1:T(8,128)} %copy-done.16, f32[768]{0:T(1024)S(1)} %fusion.40, f32[768]{0:T(1024)S(1)} %broadcast_multiply_fusion.1, f32[768]{0:T(1024)S(1)} %copy-done.95, bf16[768,3072]{1,0:T(8,128)(2,1)} %add_convert_fusion, ...), kind=kOutput, calls=%fused_computation.81 | convolution fusion | flops 3633903360 | bytes 17728512 | tf_op jit(solution)/shard_map/dot_general | solution.py:52
  158.1 5.9 convolution_convert_fusion.1
  168.1 18.7 %cross_attend_back.1 = (bf16[768,768]{1,0:T(8,128)(2,1)S(1)}, bf16[6,160,768]{2,1,0:T(8,128)(2,1)S(1)}, bf16[6,160,768]{2,1,0:T(8,128)(2,1)}) custom-call(s32[1,24]{1,0:T(1,128)S(1)} %copy-done.5, s32[1,24]{1,0:T(1,128)S(1)} %copy-done.4, bf16[160,128]{1,0:T(8,128)(2,1)S(1)} %pad.8.refs_2_, bf16[768,768]{1,0:T(8,128)(2,1)S(1)} %convolution_convert_fusion.16.refs_3_, ...), custom_call_target="tpu_custom_call" | custom-call | flops 21474836480 | bytes 12582912 | tf_op jit(solution)/shard_map/cross_attend_back/pallas_call | solution.py:312
  196.5 14.8 %self_attend_back.1 = (bf16[768,768]{1,0:T(8,128)(2,1)S(1)}, bf16[768,768]{1,0:T(8,128)(2,1)S(1)}, bf16[768,768]{1,0:T(8,128)(2,1)S(1)}) custom-call(s32[1,24]{1,0:T(1,128)S(1)} %copy-done.5, bf16[768,768]{1,0:T(8,128)(2,1)S(1)} %copy-done.11, bf16[768,768]{1,0:T(8,128)(2,1)S(1)} %copy-done.13, bf16[768,768]{1,0:T(8,128)(2,1)} %copy-done.14, ...), custom_call_target="tpu_custom_call" | custom-call | flops 21474836480 | bytes 12582912 | tf_op jit(solution)/shard_map/self_attend_back/pallas_call | solution.py:312
  269.1 26.8 %collective-permute-done.3 = bf16[960,768]{1,0:T(8,128)(2,1)S(1)} collective-permute-done((bf16[960,768]{1,0:T(8,128)(2,1)S(1)}, bf16[960,768]{1,0:T(8,128)(2,1)S(1)}, u32[]{:S(2)}, u32[]{:S(2)}) %collective-permute-start.3) | collective-permute-done | bytes 1474592 | tf_op jit(solution)/shard_map/ppermute | solution.py:28
  298.8 28.7 %collective-permute-done.2 = bf16[960,768]{1,0:T(8,128)(2,1)S(1)} collective-permute-done((bf16[960,768]{1,0:T(8,128)(2,1)S(1)}, bf16[960,768]{1,0:T(8,128)(2,1)S(1)}, u32[]{:S(2)}, u32[]{:S(2)}) %collective-permute-start.2) | collective-permute-done | bytes 1474592 | tf_op jit(solution)/shard_map/ppermute | solution.py:28
  345.9 11.2 %collective-permute-done.70 = bf16[384,768]{1,0:T(8,128)(2,1)S(1)} collective-permute-done((bf16[384,768]{1,0:T(8,128)(2,1)S(1)}, bf16[384,768]{1,0:T(8,128)(2,1)S(1)}, u32[]{:S(2)}, u32[]{:S(2)}) %collective-permute-start.70) | collective-permute-done | bytes 589856 | tf_op jit(solution)/shard_map/ppermute | solution.py:340
  359.5 5.9 collective-permute-done.80
  373.3 4.8 collective-permute-done.16
  466.3 5.1 collective-permute-done.75
  484.6 4.8 collective-permute-done.56
  506.3 5.2 collective-permute-done.93
  511.6 5.1 collective-permute-done.94
  523.7 15.1 %collective-permute-done.96 = bf16[128,768]{1,0:T(8,128)(2,1)S(1)} collective-permute-done((bf16[128,768]{1,0:T(8,128)(2,1)S(1)}, bf16[128,768]{1,0:T(8,128)(2,1)S(1)}, u32[]{:S(2)}, u32[]{:S(2)}) %collective-permute-start.96) | collective-permute-done | bytes 196640 | tf_op jit(solution)/shard_map/ppermute | solution.py:340
  549.0 6.1 collective-permute-done.77
  572.3 5.3 collective-permute-done.33
  577.7 5.3 collective-permute-done.43
  583.2 6.2 collective-permute-done.34
  589.4 5.4 collective-permute-done.44
  594.9 6.3 collective-permute-done.35
  601.6 4.8 collective-permute-done.45
  608.0 5.1 collective-permute-done.36
  614.8 5.0 collective-permute-done.46
  649.7 8.6 %maximum_maximum_fusion = f32[768,3072]{1,0:T(8,128)} fusion(f32[384,1536]{1,0:T(8,128)} %get-tuple-element.143, f32[384,1536]{1,0:T(8,128)} %get-tuple-element.142, f32[384,1536]{1,0:T(8,128)} %get-tuple-element.141, f32[384,1536]{1,0:T(8,128)} %get-tuple-element.140), kind=kLoop, calls=%fused_computation.2 | loop fusion | flops 7077888 | bytes 18874368 | tf_op jit(solution)/shard_map/concatenate | solution.py:512
  (678 shorter events, 339.5 us)
Async XLA Ops:
  6.9 36.3 %collective-permute-start = (bf16[960,768]{1,0:T(8,128)(2,1)}, bf16[960,768]{1,0:T(8,128)(2,1)S(1)}, u32[]{:S(2)}, u32[]{:S(2)}) collective-permute-start(bf16[960,768]{1,0:T(8,128)(2,1)} %convolution_convert_fusion.4), channel_id=1, source_target_pairs={{0,16},{16,0},{1,17},{17,1},{2,18},{18,2},{3,19},{19,3},{4,20},{20... | collective-permute-start | bytes 4423688 | tf_op jit(solution)/shard_map/ppermute | solution.py:28
  12.3 61.8 %collective-permute-start.1 = (bf16[960,768]{1,0:T(8,128)(2,1)}, bf16[960,768]{1,0:T(8,128)(2,1)}, u32[]{:S(2)}, u32[]{:S(2)}) collective-permute-start(bf16[960,768]{1,0:T(8,128)(2,1)} %convolution_convert_fusion.3), channel_id=1, source_target_pairs={{0,16},{16,0},{1,17},{17,1},{2,18},{18,2},{3,19},{19,3},{4,20},{20... | collective-permute-start | bytes 4423688 | tf_op jit(solution)/shard_map/ppermute | solution.py:28
  228.2 28.0 %collective-permute-start.29 = (bf16[384,1536]{1,0:T(8,128)(2,1)}, bf16[384,1536]{1,0:T(8,128)(2,1)}, u32[]{:S(2)}, u32[]{:S(2)}) collective-permute-start(bf16[384,1536]{1,0:T(8,128)(2,1)} %fusion.24), channel_id=1, source_target_pairs={{0,1},{1,0},{2,3},{3,2},{4,5},{5,4},{6,7},{7,6},{8,9},{9,8},{10,11... | collective-permute-start | bytes 3538952 | tf_op jit(solution)/shard_map/ppermute | solution.py:340
  230.0 28.8 %collective-permute-start.14 = (bf16[384,1536]{1,0:T(8,128)(2,1)}, bf16[384,1536]{1,0:T(8,128)(2,1)}, u32[]{:S(2)}, u32[]{:S(2)}) collective-permute-start(bf16[384,1536]{1,0:T(8,128)(2,1)} %fusion.29), channel_id=1, source_target_pairs={{0,1},{1,0},{2,3},{3,2},{4,5},{5,4},{6,7},{7,6},{8,9},{9,8},{10,11... | collective-permute-start | bytes 3538952 | tf_op jit(solution)/shard_map/ppermute | solution.py:340
  260.7 35.2 %collective-permute-start.3 = (bf16[960,768]{1,0:T(8,128)(2,1)S(1)}, bf16[960,768]{1,0:T(8,128)(2,1)S(1)}, u32[]{:S(2)}, u32[]{:S(2)}) collective-permute-start(bf16[960,768]{1,0:T(8,128)(2,1)S(1)} %bitcast.412), channel_id=1, source_target_pairs={{0,16},{16,0},{1,17},{17,1},{2,18},{18,2},{3,19},{19,3},{4,20},{20... | collective-permute-start | bytes 4423688 | tf_op jit(solution)/shard_map/ppermute | solution.py:28
  262.7 64.9 %collective-permute-start.2 = (bf16[960,768]{1,0:T(8,128)(2,1)S(1)}, bf16[960,768]{1,0:T(8,128)(2,1)S(1)}, u32[]{:S(2)}, u32[]{:S(2)}) collective-permute-start(bf16[960,768]{1,0:T(8,128)(2,1)S(1)} %bitcast.309), channel_id=1, source_target_pairs={{0,16},{16,0},{1,17},{17,1},{2,18},{18,2},{3,19},{19,3},{4,20},{20... | collective-permute-start | bytes 4423688 | tf_op jit(solution)/shard_map/ppermute | solution.py:28
  264.8 77.8 %collective-permute-start.30 = (bf16[192,1536]{1,0:T(8,128)(2,1)S(1)}, bf16[192,1536]{1,0:T(8,128)(2,1)S(1)}, u32[]{:S(2)}, u32[]{:S(2)}) collective-permute-start(bf16[192,1536]{1,0:T(8,128)(2,1)S(1)} %dynamic-slice_bitcast_fusion.10), channel_id=1, source_target_pairs={{0,2},{1,3},{2,0},{3,1},{4,6},{5,7},{6,4},{7,5},{8,10},{9,11},{10,... | collective-permute-start | bytes 1769480 | tf_op jit(solution)/shard_map/ppermute | solution.py:340
  266.5 77.7 %collective-permute-start.15 = (bf16[192,1536]{1,0:T(8,128)(2,1)S(1)}, bf16[192,1536]{1,0:T(8,128)(2,1)S(1)}, u32[]{:S(2)}, u32[]{:S(2)}) collective-permute-start(bf16[192,1536]{1,0:T(8,128)(2,1)S(1)} %dynamic-slice_bitcast_fusion.11), channel_id=1, source_target_pairs={{0,2},{1,3},{2,0},{3,1},{4,6},{5,7},{6,4},{7,5},{8,10},{9,11},{10,... | collective-permute-start | bytes 1769480 | tf_op jit(solution)/shard_map/ppermute | solution.py:340
  267.4 77.7 %collective-permute-start.5 = (bf16[192,1536]{1,0:T(8,128)(2,1)S(1)}, bf16[192,1536]{1,0:T(8,128)(2,1)S(1)}, u32[]{:S(2)}, u32[]{:S(2)}) collective-permute-start(bf16[192,1536]{1,0:T(8,128)(2,1)S(1)} %dynamic-slice_bitcast_fusion.12), channel_id=1, source_target_pairs={{0,16},{16,0},{1,17},{17,1},{2,18},{18,2},{3,19},{19,3},{4,20},{20... | collective-permute-start | bytes 1769480 | tf_op jit(solution)/shard_map/ppermute | solution.py:340
  296.0 49.0 %collective-permute-start.50 = (bf16[192,1536]{1,0:T(8,128)(2,1)S(1)}, bf16[192,1536]{1,0:T(8,128)(2,1)S(1)}, u32[]{:S(2)}, u32[]{:S(2)}) collective-permute-start(bf16[192,1536]{1,0:T(8,128)(2,1)S(1)} %dynamic-slice_bitcast_fusion.8), channel_id=1, source_target_pairs={{0,2},{1,3},{2,0},{3,1},{4,6},{5,7},{6,4},{7,5},{8,10},{9,11},{10,... | collective-permute-start | bytes 1769480 | tf_op jit(solution)/shard_map/ppermute | solution.py:340
  327.6 30.1 %collective-permute-start.60 = (bf16[192,1536]{1,0:T(8,128)(2,1)S(1)}, bf16[192,1536]{1,0:T(8,128)(2,1)S(1)}, u32[]{:S(2)}, u32[]{:S(2)}) collective-permute-start(bf16[192,1536]{1,0:T(8,128)(2,1)S(1)} %dynamic-slice_bitcast_fusion.7), channel_id=1, source_target_pairs={{0,16},{16,0},{1,17},{17,1},{2,18},{18,2},{3,19},{19,3},{4,20},{20... | collective-permute-start | bytes 1769480 | tf_op jit(solution)/shard_map/ppermute | solution.py:340
  344.2 21.2 %collective-permute-start.80 = (bf16[384,768]{1,0:T(8,128)(2,1)S(1)}, bf16[384,768]{1,0:T(8,128)(2,1)S(1)}, u32[]{:S(2)}, u32[]{:S(2)}) collective-permute-start(bf16[384,768]{1,0:T(8,128)(2,1)S(1)} %dynamic-slice_bitcast_fusion.5), channel_id=1, source_target_pairs={{0,16},{16,0},{1,17},{17,1},{2,18},{18,2},{3,19},{19,3},{4,20},{20... | collective-permute-start | bytes 1769480 | tf_op jit(solution)/shard_map/ppermute | solution.py:340
  345.0 77.6 %collective-permute-start.89 = (bf16[512,768]{1,0:T(8,128)(2,1)}, bf16[512,768]{1,0:T(8,128)(2,1)}, u32[]{:S(2)}, u32[]{:S(2)}) collective-permute-start(bf16[512,768]{1,0:T(8,128)(2,1)} %dynamic-slice_bitcast_fusion.4), channel_id=1, source_target_pairs={{0,1},{1,0},{2,3},{3,2},{4,5},{5,4},{6,7},{7,6},{8,9},{9,8},{10,11... | collective-permute-start | bytes 2359304 | tf_op jit(solution)/shard_map/ppermute | solution.py:340
  345.1 131.9 %collective-permute-start.39 = (bf16[384,1536]{1,0:T(8,128)(2,1)}, bf16[384,1536]{1,0:T(8,128)(2,1)}, u32[]{:S(2)}, u32[]{:S(2)}) collective-permute-start(bf16[384,1536]{1,0:T(8,128)(2,1)} %fusion.19), channel_id=1, source_target_pairs={{0,1},{1,0},{2,3},{3,2},{4,5},{5,4},{6,7},{7,6},{8,9},{9,8},{10,11... | collective-permute-start | bytes 3538952 | tf_op jit(solution)/shard_map/ppermute | solution.py:340
  357.7 20.4 %collective-permute-start.16 = (bf16[96,1536]{1,0:T(8,128)(2,1)S(1)}, bf16[96,1536]{1,0:T(8,128)(2,1)S(1)}, u32[]{:S(2)}, u32[]{:S(2)}) collective-permute-start(bf16[96,1536]{1,0:T(8,128)(2,1)S(1)} %dynamic-slice_bitcast_fusion.20), channel_id=1, source_target_pairs={{0,16},{16,0},{1,17},{17,1},{2,18},{18,2},{3,19},{19,3},{4,20},{20... | collective-permute-start | bytes 884744 | tf_op jit(solution)/shard_map/ppermute | solution.py:340
  431.6 43.9 %collective-permute-start.90 = (bf16[256,768]{1,0:T(8,128)(2,1)S(1)}, bf16[256,768]{1,0:T(8,128)(2,1)S(1)}, u32[]{:S(2)}, u32[]{:S(2)}) collective-permute-start(bf16[256,768]{1,0:T(8,128)(2,1)S(1)} %dynamic-slice_bitcast_fusion.13), channel_id=1, source_target_pairs={{0,2},{1,3},{2,0},{3,1},{4,6},{5,7},{6,4},{7,5},{8,10},{9,11},{10,... | collective-permute-start | bytes 1179656 | tf_op jit(solution)/shard_map/ppermute | solution.py:340
  471.4 19.7 %collective-permute-start.11 = (bf16[96,1536]{1,0:T(8,128)(2,1)S(1)}, bf16[96,1536]{1,0:T(8,128)(2,1)S(1)}, u32[]{:S(2)}, u32[]{:S(2)}) collective-permute-start(bf16[96,1536]{1,0:T(8,128)(2,1)S(1)} %pad_maximum_fusion.24), channel_id=1, source_target_pairs={{0,2},{1,3},{2,0},{3,1},{4,6},{5,7},{6,4},{7,5},{8,10},{9,11},{10,... | collective-permute-start | bytes 884744 | tf_op jit(solution)/shard_map/ppermute | solution.py:340
  477.0 18.7 %collective-permute-start.76 = (bf16[192,768]{1,0:T(8,128)(2,1)S(1)}, bf16[192,768]{1,0:T(8,128)(2,1)S(1)}, u32[]{:S(2)}, u32[]{:S(2)}) collective-permute-start(bf16[192,768]{1,0:T(8,128)(2,1)S(1)} %pad_maximum_fusion.30), channel_id=1, source_target_pairs={{0,16},{16,0},{1,17},{17,1},{2,18},{18,2},{3,19},{19,3},{4,20},{20... | collective-permute-start | bytes 884744 | tf_op jit(solution)/shard_map/ppermute | solution.py:340
  483.1 18.3 %collective-permute-start.86 = (bf16[192,768]{1,0:T(8,128)(2,1)S(1)}, bf16[192,768]{1,0:T(8,128)(2,1)S(1)}, u32[]{:S(2)}, u32[]{:S(2)}) collective-permute-start(bf16[192,768]{1,0:T(8,128)(2,1)S(1)} %pad_maximum_fusion.31), channel_id=1, source_target_pairs={{0,2},{1,3},{2,0},{3,1},{4,6},{5,7},{6,4},{7,5},{8,10},{9,11},{10,... | collective-permute-start | bytes 884744 | tf_op jit(solution)/shard_map/ppermute | solution.py:340
  491.0 32.0 %collective-permute-start.40 = (bf16[192,1536]{1,0:T(8,128)(2,1)S(1)}, bf16[192,1536]{1,0:T(8,128)(2,1)S(1)}, u32[]{:S(2)}, u32[]{:S(2)}) collective-permute-start(bf16[192,1536]{1,0:T(8,128)(2,1)S(1)} %dynamic-slice_bitcast_fusion.9), channel_id=1, source_target_pairs={{0,16},{16,0},{1,17},{17,1},{2,18},{18,2},{3,19},{19,3},{4,20},{20... | collective-permute-start | bytes 1769480 | tf_op jit(solution)/shard_map/ppermute | solution.py:340
  491.8 49.5 %collective-permute-start.12 = (bf16[192,1536]{1,0:T(8,128)(2,1)S(1)}, bf16[192,1536]{1,0:T(8,128)(2,1)S(1)}, u32[]{:S(2)}, u32[]{:S(2)}) collective-permute-start(bf16[192,1536]{1,0:T(8,128)(2,1)S(1)} %pad_maximum_fusion.15), channel_id=1, source_target_pairs={{0,16},{16,0},{1,17},{17,1},{2,18},{18,2},{3,19},{19,3},{4,20},{20... | collective-permute-start | bytes 1769480 | tf_op jit(solution)/shard_map/ppermute | solution.py:340
  495.7 47.3 %collective-permute-start.22 = (bf16[192,1536]{1,0:T(8,128)(2,1)S(1)}, bf16[192,1536]{1,0:T(8,128)(2,1)S(1)}, u32[]{:S(2)}, u32[]{:S(2)}) collective-permute-start(bf16[192,1536]{1,0:T(8,128)(2,1)S(1)} %pad_maximum_fusion.16), channel_id=1, source_target_pairs={{0,2},{1,3},{2,0},{3,1},{4,6},{5,7},{6,4},{7,5},{8,10},{9,11},{10,... | collective-permute-start | bytes 1769480 | tf_op jit(solution)/shard_map/ppermute | solution.py:340
  500.0 55.4 %collective-permute-start.57 = (bf16[192,1536]{1,0:T(8,128)(2,1)S(1)}, bf16[192,1536]{1,0:T(8,128)(2,1)S(1)}, u32[]{:S(2)}, u32[]{:S(2)}) collective-permute-start(bf16[192,1536]{1,0:T(8,128)(2,1)S(1)} %pad_maximum_fusion.19), channel_id=1, source_target_pairs={{0,2},{1,3},{2,0},{3,1},{4,6},{5,7},{6,4},{7,5},{8,10},{9,11},{10,... | collective-permute-start | bytes 1769480 | tf_op jit(solution)/shard_map/ppermute | solution.py:340
  521.5 22.3 %collective-permute-start.67 = (bf16[192,1536]{1,0:T(8,128)(2,1)S(1)}, bf16[192,1536]{1,0:T(8,128)(2,1)S(1)}, u32[]{:S(2)}, u32[]{:S(2)}) collective-permute-start(bf16[192,1536]{1,0:T(8,128)(2,1)S(1)} %pad_maximum_fusion.20), channel_id=1, source_target_pairs={{0,16},{16,0},{1,17},{17,1},{2,18},{18,2},{3,19},{19,3},{4,20},{20... | collective-permute-start | bytes 1769480 | tf_op jit(solution)/shard_map/ppermute | solution.py:340
  543.0 18.4 %collective-permute-start.41 = (bf16[96,1536]{1,0:T(8,128)(2,1)S(1)}, bf16[96,1536]{1,0:T(8,128)(2,1)S(1)}, u32[]{:S(2)}, u32[]{:S(2)}) collective-permute-start(bf16[96,1536]{1,0:T(8,128)(2,1)S(1)} %dynamic-slice_bitcast_fusion.18), channel_id=1, source_target_pairs={{0,2},{1,3},{2,0},{3,1},{4,6},{5,7},{6,4},{7,5},{8,10},{9,11},{10,... | collective-permute-start | bytes 884744 | tf_op jit(solution)/shard_map/ppermute | solution.py:340
  543.8 27.2 %collective-permute-start.97 = (bf16[256,768]{1,0:T(8,128)(2,1)}, bf16[256,768]{1,0:T(8,128)(2,1)}, u32[]{:S(2)}, u32[]{:S(2)}) collective-permute-start(bf16[256,768]{1,0:T(8,128)(2,1)} %pad_maximum_fusion.23), channel_id=1, source_target_pairs={{0,2},{1,3},{2,0},{3,1},{4,6},{5,7},{6,4},{7,5},{8,10},{9,11},{10,... | collective-permute-start | bytes 1179656 | tf_op jit(solution)/shard_map/ppermute | solution.py:340
  555.1 86.6 %collective-permute-start.13 = (bf16[384,1536]{1,0:T(8,128)(2,1)}, bf16[384,1536]{1,0:T(8,128)(2,1)}, u32[]{:S(2)}, u32[]{:S(2)}) collective-permute-start(bf16[384,1536]{1,0:T(8,128)(2,1)} %pad_maximum_fusion.6), channel_id=1, source_target_pairs={{0,1},{1,0},{2,3},{3,2},{4,5},{5,4},{6,7},{7,6},{8,9},{9,8},{10,11... | collective-permute-start | bytes 3538952 | tf_op jit(solution)/shard_map/ppermute | solution.py:340
  555.3 82.2 %collective-permute-start.23 = (bf16[384,1536]{1,0:T(8,128)(2,1)}, bf16[384,1536]{1,0:T(8,128)(2,1)}, u32[]{:S(2)}, u32[]{:S(2)}) collective-permute-start(bf16[384,1536]{1,0:T(8,128)(2,1)} %pad_maximum_fusion.7), channel_id=1, source_target_pairs={{0,1},{1,0},{2,3},{3,2},{4,5},{5,4},{6,7},{7,6},{8,9},{9,8},{10,11... | collective-permute-start | bytes 3538952 | tf_op jit(solution)/shard_map/ppermute | solution.py:340
  557.3 69.7 %collective-permute-start.78 = (bf16[768,768]{1,0:T(8,128)(2,1)}, bf16[768,768]{1,0:T(8,128)(2,1)}, u32[]{:S(2)}, u32[]{:S(2)}) collective-permute-start(bf16[768,768]{1,0:T(8,128)(2,1)} %pad_maximum_fusion.12), channel_id=1, source_target_pairs={{0,1},{1,0},{2,3},{3,2},{4,5},{5,4},{6,7},{7,6},{8,9},{9,8},{10,11... | collective-permute-start | bytes 3538952 | tf_op jit(solution)/shard_map/ppermute | solution.py:340
  566.7 57.8 %collective-permute-start.88 = (bf16[768,768]{1,0:T(8,128)(2,1)}, bf16[768,768]{1,0:T(8,128)(2,1)}, u32[]{:S(2)}, u32[]{:S(2)}) collective-permute-start(bf16[768,768]{1,0:T(8,128)(2,1)} %pad_maximum_fusion.13), channel_id=1, source_target_pairs={{0,1},{1,0},{2,3},{3,2},{4,5},{5,4},{6,7},{7,6},{8,9},{9,8},{10,11... | collective-permute-start | bytes 3538952 | tf_op jit(solution)/shard_map/ppermute | solution.py:340
  627.0 32.8 %collective-permute-start.37 = (bf16[192,1536]{1,0:T(8,128)(2,1)}, bf16[192,1536]{1,0:T(8,128)(2,1)}, u32[]{:S(2)}, u32[]{:S(2)}) collective-permute-start(bf16[192,1536]{1,0:T(8,128)(2,1)} %pad_maximum_fusion.17), channel_id=1, source_target_pairs={{0,2},{1,3},{2,0},{3,1},{4,6},{5,7},{6,4},{7,5},{8,10},{9,11},{10,... | collective-permute-start | bytes 1769480 | tf_op jit(solution)/shard_map/ppermute | solution.py:340
  630.4 27.9 %collective-permute-start.47 = (bf16[192,1536]{1,0:T(8,128)(2,1)}, bf16[192,1536]{1,0:T(8,128)(2,1)}, u32[]{:S(2)}, u32[]{:S(2)}) collective-permute-start(bf16[192,1536]{1,0:T(8,128)(2,1)} %pad_maximum_fusion.18), channel_id=1, source_target_pairs={{0,16},{16,0},{1,17},{17,1},{2,18},{18,2},{3,19},{19,3},{4,20},{20... | collective-permute-start | bytes 1769480 | tf_op jit(solution)/shard_map/ppermute | solution.py:340
  (189 other events, 1391.9 us)
